TPU v7x, 32 devices: a whole 2x2x4 slice. The times are simulated.
32 devices in a mesh: grp: 1, seq: 16 (over z, y, core), prm: 2 (over x), hd: 1.
Axes of the slice: x: 2, y: 2, z: 4, core: 2. Of those that a mesh axis runs over, the one named last changes fastest.
Arguments:
- query_raw: bfloat16 [2, 2048, 16, 128], P(('grp', 'prm'), 'seq', 'hd'), may hold values from -6 to 6
- key_raw: bfloat16 [2, 2048, 2, 16, 128], P(('grp', 'prm'), 'seq', None, 'hd'), may hold values from -6 to 6
- value_raw: bfloat16 [2, 2048, 2, 16, 128], P(('grp', 'prm'), 'seq', None, 'hd'), may hold values from -110 to 110
- write_rate: float32 [2, 2048, 2, 16], P(('grp', 'prm'), 'seq', None, 'hd'), may hold values from 0 to 2
- decay_rate: float32 [2, 2048, 16], P(('grp', 'prm'), 'seq', 'hd'), may hold values from 0 to 1.5
- gate_input: bfloat16 [2, 2048, 16, 128], P(('grp', 'prm'), 'seq', 'hd'), may hold values from -6 to 6
- filter_query: float32 [4, 16, 128], P(None, 'hd'), may hold values from -4 to 4
- filter_key: float32 [4, 2, 16, 128], P(None, None, 'hd'), may hold values from -4 to 4
- filter_value: float32 [4, 2, 16, 128], P(None, None, 'hd'), may hold values from -4 to 4
- output_gain: float32 [16, 128], P('hd'), may hold values from 0.25 to 1.75
Outputs:
- mixed: bfloat16 [2, 2048, 16, 128], P(('grp', 'prm'), 'seq', 'hd')
All inputs are finite; a program needn't handle non-finite values.
Results may differ from a plain program's by a relative error of at most 0.0012.
Values may be sent and summed in bfloat16 or wider, within the bound.
A program may use at most 128 MiB of HBM per device.

v0:
```python
import jax
import jax.numpy as jnp
from jax import lax
from jax.sharding import PartitionSpec as P

SPAN = 64


HIGH = lax.Precision.HIGHEST
epsilon = 1e-06


def from_behind(value, axis, by):
    count = lax.axis_size(axis)
    pairs = [(i, i + by) for i in range(count) if 0 <= i + by < count]
    return lax.ppermute(value, axis, pairs)


def prefix_2(value, axis, join, neutral):
    count, mine = (lax.axis_size(axis), lax.axis_index(axis))
    pieces = jax.tree.map(lambda part: lax.all_gather(part, axis), value)
    so_far = jax.tree.map(
        lambda part, zero: jnp.full_like(part, 0) + jnp.asarray(zero, part.dtype), value, neutral
    )

    def turn(position, so_far):
        longer = join(so_far, jax.tree.map(lambda part: part[position], pieces))
        return jax.tree.map(lambda new, old: jnp.where(position < mine, new, old), longer, so_far)

    return lax.fori_loop(0, count - 1, turn, so_far)


def short_conv(extended, kernel, tok_count):
    summed = jnp.zeros(extended[:, :tok_count].shape, jnp.float32)
    for tap_index in range(kernel.shape[0]):
        summed = summed + kernel[tap_index] * extended[:, tap_index : tap_index + tok_count].astype(
            jnp.float32
        )
    return jax.nn.silu(summed)


def unit_norm(vectors):
    return vectors / jnp.sqrt(jnp.sum(vectors * vectors, -1, keepdims=True) + epsilon)


def map_product(left_map, right_map):
    return jnp.einsum("phij,phjk->phik", left_map, right_map, precision=HIGH)


def per_device(
    query_raw,
    key_raw,
    value_raw,
    write_rate,
    decay_rate,
    gate_input,
    filter_query,
    filter_key,
    filter_value,
    output_gain,
):
    rim_size = filter_query.shape[0] - 1
    tok_count = query_raw.shape[1]
    start_rim = tok_count - rim_size
    rims = from_behind(
        (query_raw[:, start_rim:], key_raw[:, start_rim:], value_raw[:, start_rim:]), "seq", 1
    )
    queries = unit_norm(
        short_conv(jnp.concatenate([rims[0], query_raw], 1), filter_query, tok_count)
    )
    keyset = unit_norm(short_conv(jnp.concatenate([rims[1], key_raw], 1), filter_key, tok_count))
    values = short_conv(jnp.concatenate([rims[2], value_raw], 1), filter_value, tok_count)
    prompt_count = query_raw.shape[0]
    head_count = query_raw.shape[2]
    refl_count = key_raw.shape[2]
    key_dim = keyset.shape[-1]
    value_dim = values.shape[-1]
    block_count = tok_count // SPAN
    sub_steps = SPAN * refl_count

    def split_steps(source):
        shaped = source.reshape(prompt_count, block_count, sub_steps, head_count, source.shape[-1])
        return shaped.transpose(0, 1, 3, 2, 4)

    key_blocks = split_steps(keyset)
    value_blocks = split_steps(values)
    query_blocks = queries.reshape(prompt_count, block_count, SPAN, head_count, key_dim).transpose(
        0, 1, 3, 2, 4
    )
    rate_blocks = write_rate.reshape(prompt_count, block_count, sub_steps, head_count).transpose(
        0, 1, 3, 2
    )
    step_decay = jnp.concatenate(
        [
            decay_rate[:, :, None, :],
            jnp.zeros((prompt_count, tok_count, refl_count - 1, head_count), jnp.float32),
        ],
        2,
    )
    decay_blocks = step_decay.reshape(prompt_count, block_count, sub_steps, head_count).transpose(
        0, 1, 3, 2
    )
    cumulative = jnp.cumsum(decay_blocks, -1)
    row_index = lax.broadcasted_iota(jnp.int32, (sub_steps, sub_steps), 0)
    col_index = lax.broadcasted_iota(jnp.int32, (sub_steps, sub_steps), 1)
    ratio = jnp.where(
        row_index >= col_index,
        jnp.exp(jnp.minimum(cumulative[..., None, :] - cumulative[..., :, None], 0.0)),
        0.0,
    )
    gram = jnp.einsum("pchsk,pchrk->pchsr", key_blocks, key_blocks, precision=HIGH)
    lower_part = jnp.where(row_index > col_index, rate_blocks[..., :, None] * ratio * gram, 0.0)
    system = lower_part + jnp.eye(sub_steps, dtype=jnp.float32)
    decay_now = jnp.exp(-cumulative)
    right_side = jnp.concatenate(
        [(rate_blocks * decay_now)[..., None] * key_blocks, rate_blocks[..., None] * value_blocks],
        -1,
    )
    solved = lax.linalg.triangular_solve(
        system, right_side, left_side=True, lower=True, unit_diagonal=True
    )
    w_blocks = solved[..., :key_dim]
    u_blocks = solved[..., key_dim:]
    last_cum = cumulative[..., -1:]
    scaled_keys = jnp.exp(cumulative - last_cum)[..., None] * key_blocks
    eye_key = jnp.eye(key_dim, dtype=jnp.float32)
    block_a = jnp.exp(-last_cum)[..., None] * eye_key - jnp.einsum(
        "pchrk,pchrj->pchkj", scaled_keys, w_blocks, precision=HIGH
    )
    block_b = jnp.einsum("pchrk,pchrv->pchkv", scaled_keys, u_blocks, precision=HIGH)
    query_ratio = ratio[..., refl_count - 1 :: refl_count, :]
    mixing = (
        jnp.einsum("pchtk,pchrk->pchtr", query_blocks, key_blocks, precision=HIGH) * query_ratio
    )
    query_decay = decay_now[..., refl_count - 1 :: refl_count]
    p_blocks = query_decay[..., None] * query_blocks - jnp.einsum(
        "pchtr,pchrk->pchtk", mixing, w_blocks, precision=HIGH
    )
    base_out = jnp.einsum("pchtr,pchrv->pchtv", mixing, u_blocks, precision=HIGH)
    identity_map = jnp.broadcast_to(eye_key, (prompt_count, head_count, key_dim, key_dim))
    zero_state = jnp.zeros((prompt_count, head_count, key_dim, value_dim), jnp.float32)

    def compose(running, block_map):
        return (
            (
                map_product(block_map[0], running[0]),
                map_product(block_map[0], running[1]) + block_map[1],
            ),
            running,
        )

    device_map, prefixes = lax.scan(
        compose,
        (identity_map, zero_state),
        (block_a.transpose(1, 0, 2, 3, 4), block_b.transpose(1, 0, 2, 3, 4)),
    )

    def combine(earlier, later_map):
        return (
            map_product(later_map[0], earlier[0]),
            map_product(later_map[0], earlier[1]) + later_map[1],
        )

    prefix = prefix_2((device_map[0], device_map[1]), "seq", combine, (identity_map, zero_state))
    state_in = prefix[1]
    block_in = jnp.einsum("cphij,phjv->cphiv", prefixes[0], state_in, precision=HIGH) + prefixes[1]
    block_in = block_in.transpose(1, 0, 2, 3, 4)
    out_blocks = jnp.einsum("pchtk,pchkv->pchtv", p_blocks, block_in, precision=HIGH) + base_out
    outputs = out_blocks.transpose(0, 1, 3, 2, 4).reshape(
        prompt_count, tok_count, head_count, value_dim
    )
    normed = outputs / jnp.sqrt(jnp.mean(outputs * outputs, -1, keepdims=True) + epsilon)
    return (normed * output_gain * jax.nn.silu(gate_input.astype(jnp.float32))).astype(jnp.bfloat16)


def solution(mesh):
    return jax.shard_map(
        per_device,
        mesh=mesh,
        in_specs=(
            P(("grp", "prm"), "seq", "hd", None),
            P(("grp", "prm"), "seq", None, "hd", None),
            P(("grp", "prm"), "seq", None, "hd", None),
            P(("grp", "prm"), "seq", None, "hd"),
            P(("grp", "prm"), "seq", "hd"),
            P(("grp", "prm"), "seq", "hd", None),
            P(None, "hd", None),
            P(None, None, "hd", None),
            P(None, None, "hd", None),
            P("hd", None),
        ),
        out_specs=P(("grp", "prm"), "seq", "hd", None),
        check_vma=False,
    )
```

profile of v0, /device:TPU:29, one launch (start us, length us, event | category | flops | bytes accessed | tf_op | source)
XLA Modules:
  0.0 700.7 jit_solution(7430603232891163755)
XLA Ops:
  6.5 0.9 slice.110
  7.4 1.3 collective-permute-start.2
  8.7 0.7 slice.101
  9.5 1.3 collective-permute-start.1
  10.9 0.8 copy.94
  11.8 0.6 reduce_window_sum.11
  12.6 0.8 slice_bitcast_fusion.27
  13.4 0.8 slice_bitcast_fusion.23
  14.2 0.8 copy.60
  15.4 0.6 constant_dynamic-update-slice_fusion.6
  16.0 1.1 constant_dynamic-update-slice_fusion.5
  17.1 1.2 multiply_reduce_fusion
  18.5 0.7 broadcast_divide_fusion
  19.3 7.2 %add_bitcast_fusion = f32[1,2,16,1,128,128]{5,4,3,2,1,0:T(8,128)} fusion(f32[1,2,128,16,128]{4,3,2,1,0:T(8,128)S(1)} %bitcast.242, f32[128,128]{1,0:T(8,128)S(1)} %fusion.77, f32[128,128]{1,0:T(8,128)S(1)} %get-tuple-element.249, f32[2,16,128]{2,1,0:T(8,128)S(1)} %bitcast.253, f32[2,16,128]{2,1,0:T(8,128)S(1)} %bitcast.258, ...), kind=kOutput, calls=%fused_computation.51 | convolution fusion | flops 810024960 | bytes 4407296 | tf_op jit(solution)/shard_map/pchsk,pchrk->pchsr/dot_general | solution.py:111
  26.5 316.3 %custom-call.3 = f32[1,2,16,1,128,128]{4,5,3,2,1,0:T(8,128)} custom-call(f32[1,2,16,1,128,128]{5,4,3,2,1,0:T(8,128)} %add_bitcast_fusion), custom_call_target="InvertDiagBlocksLowerTriangular" | custom-call | tf_op jit(solution)/shard_map/triangular_solve | solution.py:119
  342.8 3.2 divide_multiply_fusion
  346.0 1.5 bitcast_multiply_fusion
  347.6 3.8 fusion.22
  351.4 5.6 fusion.41
  357.0 5.9 subtract_bitcast_fusion
  363.1 17.5 %while.30 = (s32[]{:T(128)}, f32[1,16,128,128]{3,2,1,0:T(8,128)S(1)}, f32[1,16,128,128]{3,2,1,0:T(8,128)S(1)}, f32[2,1,16,128,128]{4,3,2,1,0:T(8,128)}, f32[2,1,...) while((s32[]{:T(128)}, ...), condition=%wide.region_4.5_spmd, body=%wide.region_3.4_spmd.sunk | while | flops 805568512 | bytes 63964432 | solution.py:152
  363.6 3.9 fusion.96
  367.7 2.1 copy-done
  369.9 1.2 convolution_bitcast_fusion.2
  371.2 0.6 copy-done.4
  372.4 3.9 fusion.96
  376.5 2.1 copy-done
  378.6 1.2 convolution_bitcast_fusion.2
  379.9 0.6 copy-done.4
  380.6 1.0 copy-done.3
  381.9 0.4 all-gather.7.cloned.1.call-update
  382.3 0.7 slice.93
  383.0 1.3 collective-permute-start
  384.3 0.6 exponential_select_fusion
  385.0 0.3 slice.91
  385.3 3.0 slice.108
  388.3 1.1 constant_dynamic-update-slice_fusion.1
  389.5 1.8 multiply_reduce_fusion.2
  391.3 0.4 broadcast_divide_fusion.1
  391.7 4.6 fusion.61
  396.4 2.4 fusion.65
  398.7 110.2 %all-gather.5.cloned.1.call-done = f32[16,16,128,128]{3,2,1,0:T(8,128)} async-done(((f32[1,16,128,128]{3,2,1,0:T(8,128)}), f32[16,16,128,128]{3,2,1,0:T(8,128)}) %all-gather.5.cloned.1.call-update) | async-done | bytes 16777232 | tf_op jit(solution)/shard_map/all_gather | solution.py:21
  508.9 127.3 %all-gather.7.cloned.1.call-done = f32[16,16,128,128]{3,2,1,0:T(8,128)} async-done(((f32[1,16,128,128]{3,2,1,0:T(8,128)}), f32[16,16,128,128]{3,2,1,0:T(8,128)}) %all-gather.7.cloned.1.call-update) | async-done | bytes 16777232 | tf_op jit(solution)/shard_map/all_gather | solution.py:21
  636.2 44.3 %while.31 = (s32[]{:T(128)}, f32[1,16,128,128]{3,2,1,0:T(8,128)S(1)}, s32[]{:T(128)}, f32[16,1,16,128,128]{4,3,2,1,0:T(8,128)}, f32[16,1,16,128,128]{4,3,2,1,0:T(8,128)}, /*index=5*/s32[]{:T(128)}, s32[]{:T(128)}) while((s32[]{:T(128)}, f32[1,16,128,128]{3,2,1,0:T(8,128)S(1)}, s32[]{:T(128)}, f32[16,1,16,128,128]{4,3,2,1,0:T(8,128)}, ...), condition=%wide.region_6.7_spmd.clone, body=%wide.region_5.6_spmd.clone.sunk | while | flops 403701760 | bytes 7342695 | solution.py:30
  636.3 2.8 fusion.99
  639.2 2.8 fusion.99
  642.1 2.8 fusion.99
  645.1 2.8 fusion.99
  648.0 2.8 fusion.99
  650.9 2.8 fusion.99
  653.8 2.8 fusion.99
  656.8 2.9 fusion.99
  659.8 2.9 fusion.99
  662.8 2.8 fusion.99
  665.7 2.8 fusion.99
  668.7 2.8 fusion.99
  671.6 2.8 fusion.99
  674.5 2.8 fusion.99
  677.5 2.8 fusion.99
  680.5 4.3 fusion.23
  684.8 4.2 fusion.24
  689.0 2.2 multiply_reduce_fusion.1
  691.4 0.6 copy.74
  692.3 1.3 fusion.74
  (103 shorter events, 4.8 us)
Async XLA Ops:
  6.5 8.6 %copy-start.9 = (bf16[1,128,2,16,128]{4,3,2,1,0:T(8,128)(2,1)S(1)}, bf16[1,128,2,16,128]{4,3,2,1,0:T(8,128)(2,1)}, u32[]{:S(2)}) copy-start(bf16[1,128,2,16,128]{4,3,2,1,0:T(8,128)(2,1)} %param.15) | copy-start | bytes 3145732
  6.5 9.4 %copy-start.10 = (bf16[1,128,2,16,128]{4,3,2,1,0:T(8,128)(2,1)S(1)}, bf16[1,128,2,16,128]{4,3,2,1,0:T(8,128)(2,1)}, u32[]{:S(2)}) copy-start(bf16[1,128,2,16,128]{4,3,2,1,0:T(8,128)(2,1)} %param.16) | copy-start | bytes 3145732
  6.5 502.4 %all-gather.5.cloned.1.call-start = ((), (), s32[]{:S(2)}) async-start(), calls=%async_computation | async-start | bytes 17825792 | tf_op jit(solution)/shard_map/all_gather | solution.py:21
  7.4 7.9 %collective-permute-start.2 = (bf16[1,3,2,16,128]{4,3,2,1,0:T(8,128)(2,1)S(1)}, bf16[1,3,2,16,128]{4,3,2,1,0:T(8,128)(2,1)S(1)}, u32[]{:S(2)}, u32[]{:S(2)}) collective-permute-start(bf16[1,3,2,16,128]{4,3,2,1,0:T(8,128)(2,1)S(1)} %slice.110), channel_id=1, source_target_pairs={{0,2},{2,4},{4,6},{6,8},{8,10},{10,12},{12,14},{14,16},{16,18},{18... | collective-permute-start | bytes 73736 | tf_op jit(solution)/shard_map/ppermute | solution.py:16
  9.5 5.7 collective-permute-start.1
  19.2 337.7 %copy-start.1 = (f32[1,128,2,16,128]{4,3,2,1,0:T(8,128)}, f32[1,128,2,16,128]{4,3,2,1,0:T(8,128)S(1)}, u32[]{:S(2)}) copy-start(f32[1,128,2,16,128]{4,3,2,1,0:T(8,128)S(1)} %broadcast_divide_fusion) | copy-start | bytes 6291460
  19.2 323.6 %copy-start.11 = (bf16[1,128,2,16,128]{4,3,2,1,0:T(8,128)(2,1)S(1)}, bf16[1,128,2,16,128]{4,3,2,1,0:T(8,128)(2,1)}, u32[]{:S(2)}) copy-start(bf16[1,128,2,16,128]{4,3,2,1,0:T(8,128)(2,1)} %param.16) | copy-start | bytes 3145732
  346.0 1.6 copy-start.17
  351.4 5.6 copy-start.6
  363.6 3.9 copy-start.13
  363.6 4.0 copy-start.15
  367.5 2.3 copy-start
  367.6 3.4 copy-start.14
  369.9 1.4 copy-start.16
  369.9 2.0 copy-start.4
  372.4 3.9 copy-start.13
  372.4 4.0 copy-start.15
  376.2 2.3 copy-start
  376.3 3.4 copy-start.14
  378.6 1.4 copy-start.16
  378.6 2.0 copy-start.4
  380.6 1.0 copy-start.3
  380.6 1.3 copy-start.5
  380.6 4.4 copy-start.19
  381.6 254.6 %all-gather.7.cloned.1.call-start = ((), (), s32[]{:S(2)}) async-start(), calls=%async_computation.1 | async-start | bytes 17825792 | tf_op jit(solution)/shard_map/all_gather | solution.py:21
  383.0 5.3 collective-permute-start
  389.5 2.2 copy-start.2
  389.5 2.2 copy-start.12
  391.7 4.7 copy-start.7
  684.8 4.2 copy-start.8
  691.3 1.0 copy-start.18
  691.3 1.0 copy-start.20
Sparse Core Ops, SparseCore 0:
  381.7 127.2 all-gather.4
  511.1 125.0 all-gather.6
where the time goes:
time: 711 us; the launch traced here: 701 us
  other arithmetic  328 us (46%)
  waiting for transfers between devices  238 us (33%)
  matrix products  92.7 us (13%)
  local copies, waits for them, and re-layouts  22.9 us (3%)
  between operations  14.1 us (2%)
    another operation x3, other arithmetic, per_device(): lax.linalg.triangular_solve(system, right_side, left_side=True, lower=Tru...  316 us
    all_gather x2, waiting for transfers between devices, prefix_2(): pieces = jax.tree.map(lambda part: lax.all_gather(part, axis), value)  237 us
    dot_general x19, matrix products, map_product(): return jnp.einsum('phij,phjk->phik', left_map, right_map, precision=HIGH)  52.5 us
  transfers between devices with their start and end apart: 5, of which 2 were waited for; matrix products, arithmetic and copies ran while one was open for 3% of the time, Pallas kernels for 0%

commit v1 on v0

v1 whole, which is shorter than its diff:
```python
import functools

import jax
import jax.numpy as jnp
from jax import lax
from jax.experimental import pallas as pl
from jax.experimental.pallas import tpu as pltpu
from jax.sharding import PartitionSpec as P

HIGH = lax.Precision.HIGHEST
epsilon = 1e-06
CHUNK = 4
GROUP = 4
F32 = jnp.float32
BF16 = jnp.bfloat16


def split(x):
    hi = x.astype(BF16)
    return hi, (x - hi.astype(F32)).astype(BF16)


def dot(a, b):
    return jnp.dot(a, b, preferred_element_type=F32)


def dot_nt(a, b):
    return lax.dot_general(a, b, (((1,), (1,)), ((), ())), preferred_element_type=F32)


def pair(x):
    return jnp.concatenate(split(x), 1)


def mm_square(left_pair, right):
    rows = pair(right)
    out = dot(left_pair, jnp.concatenate([rows, rows], 0))
    width = right.shape[1]
    return out[:, :width] + out[:, width:]


def mm_wide(left, right):
    left_hi, left_lo = split(left)
    hi, lo = split(right)
    both = jnp.concatenate([left_hi, left_lo], 1)
    return dot(both, jnp.concatenate([hi, hi], 0)) + dot(left_hi, lo)


def mm_deep(left, right):
    left_hi, left_lo = split(left)
    hi, lo = split(right)
    return dot(left_hi, hi) + (dot(left_lo, hi) + dot(left_hi, lo))


def conv_into(x_ref, rim_ref, filter_ref, buf, normalize):
    taps = filter_ref.shape[0]
    rim = taps - 1
    tok = x_ref.shape[0]
    rows = CHUNK * (buf.shape[0] // tok)

    def finish(window, start):
        summed = jnp.zeros((CHUNK,) + window.shape[1:], F32)
        for tap in range(taps):
            summed = summed + filter_ref[tap] * window[tap : tap + CHUNK]
        out = jax.nn.silu(summed)
        if normalize:
            out = out / jnp.sqrt(jnp.sum(out * out, -1, keepdims=True) + epsilon)
        buf[pl.ds(start, rows), :] = out.reshape(rows, out.shape[-1])

    finish(
        jnp.concatenate([rim_ref[...].astype(F32), x_ref[0:CHUNK].astype(F32)], 0), 0
    )

    @pl.loop(1, tok // CHUNK)
    def _(step):
        window = x_ref[pl.ds(step * CHUNK - rim, CHUNK + rim)].astype(F32)
        finish(window, pl.multiple_of(step * rows, rows))


def local_kernel(
    q_ref, k_ref, v_ref, rq_ref, rk_ref, rv_ref, fq_ref, fk_ref, fv_ref,
    cum_ref, rate_ref, tok_ref, row_ref,
    pb_ref, ab_ref, q_buf, k_buf, v_buf,
):
    heads = q_ref.shape[1]
    tok = q_ref.shape[0]
    refl = k_ref.shape[1]
    steps = tok * refl
    group = pb_ref.shape[0]

    @pl.when(pl.program_id(0) == 0)
    def _():
        conv_into(q_ref, rq_ref, fq_ref, q_buf, True)
        conv_into(k_ref, rk_ref, fk_ref, k_buf, True)
        conv_into(v_ref, rv_ref, fv_ref, v_buf, False)

    half = steps // 2
    row = lax.broadcasted_iota(jnp.int32, (half, half), 0)
    col = lax.broadcasted_iota(jnp.int32, (half, half), 1)
    qrow = lax.broadcasted_iota(jnp.int32, (tok, steps), 0)
    qcol = lax.broadcasted_iota(jnp.int32, (tok, steps), 1)
    eye = jnp.where(row == col, 1.0, 0.0)
    dim = q_ref.shape[2]
    drow = lax.broadcasted_iota(jnp.int32, (dim, dim), 0)
    dcol = lax.broadcasted_iota(jnp.int32, (dim, dim), 1)

    work = []
    for g in range(group):
        head = pl.program_id(0) * group + g
        K = k_buf[pl.ds(head, steps, stride=heads), :]
        V = v_buf[pl.ds(head, steps, stride=heads), :]
        Q = q_buf[pl.ds(head, tok, stride=heads), :]
        cum = cum_ref[0, :, g : g + 1]
        rate = rate_ref[0, :, g : g + 1]
        cum_tok = tok_ref[0, :, g : g + 1]
        cum_row = row_ref[0, g : g + 1, :]
        last = cum_row[:, steps - 1 : steps]
        k_hi, k_lo = split(K)
        q_hi, q_lo = split(Q)
        hi = jnp.concatenate([k_hi, q_hi], 0)
        lo = jnp.concatenate([k_lo, q_lo], 0)
        gram = dot_nt(
            jnp.concatenate([hi, lo], 1), jnp.concatenate([k_hi, k_hi], 1)
        ) + dot_nt(hi, k_lo)

        def lower(r, c):
            ratio = jnp.exp(
                jnp.minimum(cum_row[:, c * half : (c + 1) * half] - cum[r * half : (r + 1) * half], 0.0)
            )
            block = gram[r * half : (r + 1) * half, c * half : (c + 1) * half]
            value = rate[r * half : (r + 1) * half] * ratio * block
            return jnp.where(row > col, value, 0.0) if r == c else value

        low = [lower(0, 0), lower(1, 1)]
        low_21 = lower(1, 0)
        mixing = jnp.where(
            qrow * refl + (refl - 1) >= qcol,
            gram[steps:] * jnp.exp(jnp.minimum(cum_row - cum_tok, 0.0)),
            0.0,
        )
        right = jnp.concatenate([(rate * jnp.exp(-cum)) * K, rate * V], 1)
        keys_t = K.T * jnp.exp(cum_row - last)
        work.append((low, low_21, mixing, right, keys_t, Q, cum_tok, last))

    inverse = [
        [eye - jnp.where((row // 2) == (col // 2), low, 0.0) for low in item[0]] for item in work
    ]
    size = 2
    while size < half:
        mask = ((row // (2 * size)) == (col // (2 * size))) & ((row // size) != (col // size))
        lefts = [[pair(x) for x in two] for two in inverse]
        inner = [
            [
                mm_square(pair(jnp.where(mask, low, 0.0)), x)
                for low, x in zip(item[0], two)
            ]
            for item, two in zip(work, inverse)
        ]
        inverse = [
            [x - mm_square(l, y) for x, l, y in zip(two, ls, ys)]
            for two, ls, ys in zip(inverse, lefts, inner)
        ]
        size *= 2

    for g, (item, two) in enumerate(zip(work, inverse)):
        low, low_21, mixing, right, keys_t, Q, cum_tok, last = item
        top = mm_wide(two[0], right[:half])
        bottom = mm_wide(two[1], right[half:] - mm_wide(low_21, top))
        solved = jnp.concatenate([top, bottom], 0)
        ab = mm_deep(keys_t, solved)
        pb = mm_deep(mixing, solved)
        ab_ref[g, :, :dim] = jnp.where(drow == dcol, jnp.exp(-last), 0.0) - ab[:, :dim]
        ab_ref[g, :, dim:] = ab[:, dim:]
        pb_ref[g, :, :dim] = jnp.exp(-cum_tok) * Q - pb[:, :dim]
        pb_ref[g, :, dim:] = pb[:, dim:]


def chain_kernel(ab_ref, s_ref, recv, send, send_sem, recv_sem):
    count = lax.axis_size("seq")
    me = lax.axis_index("seq")
    right = lax.rem(me + 1, count)
    left = lax.rem(me + count - 1, count)
    heads, dim = ab_ref.shape[0], ab_ref.shape[1]
    barrier = pltpu.get_barrier_semaphore()

    @pl.when(me > 0)
    def _():
        pl.semaphore_signal(
            barrier, inc=1, device_id={"seq": left}, device_id_type=pl.DeviceIdType.MESH
        )

    @pl.when(me < count - 1)
    def _():
        pl.semaphore_signal(
            barrier, inc=1, device_id={"seq": right}, device_id_type=pl.DeviceIdType.MESH
        )

    pl.semaphore_wait(barrier, jnp.minimum(me, 1) + jnp.minimum(count - 1 - me, 1))

    def copy(h):
        return pltpu.make_async_remote_copy(
            src_ref=send.at[h],
            dst_ref=recv.at[h],
            send_sem=send_sem.at[h],
            recv_sem=recv_sem.at[h],
            device_id={"seq": right},
            device_id_type=pl.DeviceIdType.MESH,
        )

    @pl.when(me == 0)
    def _():
        recv[...] = jnp.zeros_like(recv)

    @pl.loop(0, heads)
    def _(h):
        left_pair = pair(ab_ref[h, :, :dim])

        @pl.when(me > 0)
        def _():
            copy(h).wait_recv()

        state = recv[h]

        @pl.when(me < count - 1)
        def _():
            send[h] = mm_square(left_pair, state) + ab_ref[h, :, dim:]
            copy(h).start()

        s_ref[h] = state

    @pl.when(me < count - 1)
    def _():
        @pl.loop(0, heads)
        def _(h):
            copy(h).wait_send()


def out_kernel(pb_ref, s_ref, gate_ref, gain_ref, out_ref, buf):
    heads, tok, dim = pb_ref.shape[0], pb_ref.shape[1], pb_ref.shape[2] // 2

    @pl.loop(0, heads // GROUP)
    def _(step):
        for g in range(GROUP):
            h = step * GROUP + g
            value = mm_square(pair(pb_ref[h, :, :dim]), s_ref[h]) + pb_ref[h, :, dim:]
            buf[pl.ds(h, tok, stride=heads), :] = value

    rows = 8 * heads

    @pl.loop(0, tok // 8)
    def _(step):
        value = buf[pl.ds(pl.multiple_of(step * rows, rows), rows), :].reshape(8, heads, dim)
        normed = value / jnp.sqrt(jnp.mean(value * value, -1, keepdims=True) + epsilon)
        gate = jax.nn.silu(gate_ref[pl.ds(step * 8, 8)].astype(F32))
        out_ref[pl.ds(step * 8, 8)] = (normed * gain_ref[...] * gate).astype(out_ref.dtype)


VMEM = pl.BlockSpec(memory_space=pltpu.VMEM)


def one_prompt(q, k, v, rate, decay, gate, rims, fq, fk, fv, gain):
    tok, heads, dim = q.shape
    refl = k.shape[1]
    steps = tok * refl
    group = GROUP
    parts = heads // group
    order = lax.broadcasted_iota(jnp.int32, (tok, tok), 0) >= lax.broadcasted_iota(
        jnp.int32, (tok, tok), 1
    )
    cum = jnp.dot(order.astype(F32), decay, precision=HIGH)
    cum_steps = jnp.repeat(cum, refl, axis=0)

    def columns(x):
        return x.reshape(x.shape[0], parts, group).transpose(1, 0, 2)

    def whole(shape):
        return pl.BlockSpec(shape, lambda i: (0,) * len(shape))

    def part(shape):
        return pl.BlockSpec((1,) + shape, lambda i: (i, 0, 0))

    args = (
        q, k, v, rims[:, 0], rims[:, 1 : 1 + refl], rims[:, 1 + refl :], fq, fk, fv,
        columns(cum_steps), columns(rate.reshape(steps, heads)), columns(cum),
        cum_steps.T.reshape(parts, group, steps),
    )
    pb, ab = pl.pallas_call(
        local_kernel,
        grid=(parts,),
        in_specs=[whole(x.shape) for x in args[:9]]
        + [part((steps, group)), part((steps, group)), part((tok, group)), part((group, steps))],
        out_specs=[
            pl.BlockSpec((group, tok, 2 * dim), lambda i: (i, 0, 0)),
            pl.BlockSpec((group, dim, 2 * dim), lambda i: (i, 0, 0)),
        ],
        out_shape=[
            jax.ShapeDtypeStruct((heads, tok, 2 * dim), F32),
            jax.ShapeDtypeStruct((heads, dim, 2 * dim), F32),
        ],
        scratch_shapes=[
            pltpu.VMEM((tok * heads, dim), F32),
            pltpu.VMEM((steps * heads, dim), F32),
            pltpu.VMEM((steps * heads, dim), F32),
        ],
        compiler_params=pltpu.CompilerParams(vmem_limit_bytes=48 * 2**20),
    )(*args)
    states = pl.pallas_call(
        chain_kernel,
        in_specs=[VMEM],
        out_specs=VMEM,
        out_shape=jax.ShapeDtypeStruct((heads, dim, dim), F32),
        scratch_shapes=[
            pltpu.VMEM((heads, dim, dim), F32),
            pltpu.VMEM((heads, dim, dim), F32),
            pltpu.SemaphoreType.DMA((heads,)),
            pltpu.SemaphoreType.DMA((heads,)),
        ],
        compiler_params=pltpu.CompilerParams(
            collective_id=0, has_side_effects=True, vmem_limit_bytes=32 * 2**20
        ),
    )(ab)
    return pl.pallas_call(
        out_kernel,
        in_specs=[VMEM] * 4,
        out_specs=VMEM,
        out_shape=jax.ShapeDtypeStruct((tok, heads, dim), BF16),
        scratch_shapes=[pltpu.VMEM((tok * heads, dim), F32)],
        compiler_params=pltpu.CompilerParams(vmem_limit_bytes=32 * 2**20),
    )(pb, states, gate, gain)


def per_device(
    query_raw,
    key_raw,
    value_raw,
    write_rate,
    decay_rate,
    gate_input,
    filter_query,
    filter_key,
    filter_value,
    output_gain,
):
    rim_size = filter_query.shape[0] - 1
    start = query_raw.shape[1] - rim_size
    count = lax.axis_size("seq")
    edge = jnp.concatenate(
        [query_raw[:, start:, None], key_raw[:, start:], value_raw[:, start:]], 2
    )
    rims = lax.ppermute(edge, "seq", [(i, i + 1) for i in range(count - 1)])
    return jnp.stack(
        [
            one_prompt(
                query_raw[p], key_raw[p], value_raw[p], write_rate[p], decay_rate[p],
                gate_input[p], rims[p], filter_query, filter_key, filter_value, output_gain,
            )
            for p in range(query_raw.shape[0])
        ]
    )


def solution(mesh):
    return jax.shard_map(
        per_device,
        mesh=mesh,
        in_specs=(
            P(("grp", "prm"), "seq", "hd", None),
            P(("grp", "prm"), "seq", None, "hd", None),
            P(("grp", "prm"), "seq", None, "hd", None),
            P(("grp", "prm"), "seq", None, "hd"),
            P(("grp", "prm"), "seq", "hd"),
            P(("grp", "prm"), "seq", "hd", None),
            P(None, "hd", None),
            P(None, None, "hd", None),
            P(None, None, "hd", None),
            P("hd", None),
        ),
        out_specs=P(("grp", "prm"), "seq", "hd", None),
        check_vma=False,
    )
```

time: 711 us -> 97.1 us (0.14); the launches traced: 701 us -> 96.4 us
  other arithmetic: 328 us -> 0.62 us
  waiting for transfers between devices: 238 us -> 0.01 us
  matrix products: 92.7 us -> 0.12 us
  Pallas kernels: 0 us -> 81 us
  between operations: 14.1 us -> 0.15 us
  local copies, waits for them, and re-layouts: 22.9 us -> 13.2 us
    another operation x6 -> x0, other arithmetic: 317 us -> none  [the longest x3 316 us: per_device(): lax.linalg.triangular_solve(system, right_side, left_side=True, lower=Tru...]
    all_gather x2 -> x0, waiting for transfers between devices: 237 us -> none  [prefix_2(): pieces = jax.tree.map(lambda part: lax.all_gather(part, axis), value)]
    dot_general x27 -> x1, matrix products: 88.9 us -> 0.12 us  [one_prompt(): cum = jnp.dot(order.astype(F32), decay, precision=HIGH)]
    pallas_call x0 -> x3, Pallas kernels: none -> 81 us  [the longest x1 43 us: one_prompt(): pl.pallas_call(chain_kernel, in_specs=[VMEM], out_specs=VMEM, out_shape=j...]
    while x43 -> x0, local copies, waits for them, and re-layouts: 7.25 us -> none
  transfers between devices with their start and end apart: 5 -> 1, of which waited for: 2 -> 0; matrix products, arithmetic and copies ran while one was open for 3% -> 6% of each run, Pallas kernels for 0% -> 0%
where the time goes in v1:
time: 97.1 us; the launch traced here: 96.4 us
  Pallas kernels  81 us (83%)
  local copies, waits for them, and re-layouts  13.2 us (14%)
  starting transfers between devices  1.28 us (1%)
    pallas_call x1, Pallas kernels, one_prompt(): pl.pallas_call(chain_kernel, in_specs=[VMEM], out_specs=VMEM, out_shape=j...  43 us
    pallas_call x1, Pallas kernels, one_prompt(): pl.pallas_call(local_kernel, grid=(parts,), in_specs=[whole(x.shape) for...  34.2 us
    unnamed x25, local copies, waits for them, and re-layouts  4.98 us
    pallas_call x1, Pallas kernels, one_prompt(): pl.pallas_call(out_kernel, in_specs=[VMEM] * 4, out_specs=VMEM, out_shape...  3.76 us
    another operation x2, local copies, waits for them, and re-layouts, columns(): return x.reshape(x.shape[0], parts, group).transpose(1, 0, 2)  2.2 us
  transfers between devices with their start and end apart: 1, of which 0 were waited for; matrix products, arithmetic and copies ran while one was open for 6% of the time, Pallas kernels for 0%

profile of v1, /device:TPU:29, one launch (start us, length us, event | category | flops | bytes accessed | tf_op | source)
XLA Modules:
  0.0 96.4 jit_solution(4605953274267975535)
XLA Ops:
  0.0 0.0 copy-start
  0.0 0.7 slice_bitcast_fusion.1
  0.7 0.7 slice.19
  1.5 0.7 slice.20
  2.2 0.6 pad_maximum_fusion
  2.8 1.3 %collective-permute-start = (bf16[1,3,5,16,128]{4,3,2,1,0:T(8,128)(2,1)}, bf16[1,3,5,16,128]{4,3,2,1,0:T(8,128)(2,1)}, u32[]{:S(2)}, u32[]{:S(2)}) collective-permute-start(bf16[1,3,5,16,128]{4,3,2,1,0:T(8,128)(2,1)} %pad_maximum_fusion), channel_id=1, source_target_pairs={{0,2},{2,4},{4,6},{6,8},{8,10},{10,12},{12,14},{14,16},{16,18},{18... | collective-permute-start | bytes 184328 | tf_op jit(solution)/shard_map/ppermute | solution.py:350
  4.1 0.0 copy-done
  4.1 0.1 fusion
  4.3 0.2 copy.11
  4.4 0.8 copy.13
  5.3 0.0 copy-start.3
  5.3 0.0 copy-start.4
  5.3 0.0 copy-start.7
  5.3 0.0 copy-start.8
  5.3 1.1 %reshape_reshape_squeeze.3 = f32[256,4,4]{2,1,0:T(4,128)} reshape(f32[1,128,2,16]{3,2,1,0:T(2,128)S(1)} %copy.13) | data formatting | bytes 32768 | tf_op jit(solution)/shard_map/reshape;reshape;squeeze | solution.py:274
  6.5 1.1 %reshape_reshape.3 = f32[256,4,4]{2,1,0:T(4,128)} reshape(f32[128,2,16]{2,1,0:T(2,128)S(1)} %broadcast_in_dim.7) | data formatting | bytes 32768 | tf_op jit(solution)/shard_map/reshape;reshape | solution.py:274
  7.5 1.3 %copy_bitcast_fusion = (f32[4,256,4]{2,1,0:T(8,128)S(1)}, f32[4,256,4]{2,1,0:T(8,128)S(1)}) fusion(f32[256,4,4]{2,1,0:T(4,128)} %reshape_reshape_squeeze.3, f32[256,4,4]{2,1,0:T(4,128)} %reshape_reshape.3), kind=kLoop, calls=%fused_computation | loop fusion | bytes 65536 | tf_op jit(solution)/shard_map/transpose | solution.py:274
  8.8 0.1 copy.16
  8.9 0.6 reshape.11.row_ref
  9.5 0.1 copy.15
  9.7 0.0 collective-permute-done
  9.7 0.7 slice_bitcast_fusion.rq_ref
  10.4 0.8 fusion.2
  11.1 0.0 copy-done.3
  11.1 0.0 copy-done.4
  11.2 0.0 copy-done.7
  11.2 0.0 copy-done.8
  11.2 0.0 copy-start.5
  11.2 1.0 %copy-done.5 = bf16[1,128,16,128]{3,2,1,0:T(8,128)(2,1)S(1)} copy-done((bf16[1,128,16,128]{3,2,1,0:T(8,128)(2,1)S(1)}, bf16[1,128,16,128]{3,2,1,0:T(8,128)(2,1)}, u32[]{:S(2)}) %copy-start.5) | copy-done | bytes 524312
  12.2 0.0 copy-start.9
  12.2 0.7 copy-done.9
  12.9 0.0 copy-start.10
  12.9 0.8 copy-done.10
  13.7 34.2 %shard_map.100 = (f32[16,128,256]{2,1,0:T(8,128)}, f32[16,128,256]{2,1,0:T(8,128)}) custom-call(bf16[128,16,128]{2,1,0:T(8,128)(2,1)S(1)} %bitcast.25, bf16[128,2,16,128]{3,2,1,0:T(8,128)(2,1)S(1)} %bitcast.22, bf16[128,2,16,128]{3,2,1,0:T(8,128)(2,1)S(1)} %bitcast.23, bf16[3,16,128]{2,1,0:T(8,128)(2,1)S(1)} %slice_bitcast_fusion.rq_ref, ...), custom_call_target="tpu_custom_call" | custom-call | tf_op jit(solution)/shard_map/pallas_call | solution.py:287
  47.9 0.0 copy-start.1
  47.9 1.6 %copy-done.1 = f32[16,128,256]{2,1,0:T(8,128)S(1)} copy-done((f32[16,128,256]{2,1,0:T(8,128)S(1)}, f32[16,128,256]{2,1,0:T(8,128)}, u32[]{:S(2)}) %copy-start.1) | copy-done | bytes 2097176
  49.5 0.0 copy-start.2
  49.5 0.0 copy-start.6
  49.5 0.0 copy-start.11
  49.5 43.0 %shard_map.101.s_ref = f32[16,128,128]{2,1,0:T(8,128)S(1)} custom-call(f32[16,128,256]{2,1,0:T(8,128)S(1)} %copy-done.1), custom_call_target="tpu_custom_call" | custom-call | tf_op jit(solution)/shard_map/pallas_call | solution.py:307
  92.6 0.0 copy-done.2
  92.6 0.0 copy-done.6
  92.6 0.0 copy-done.11
  92.6 3.8 %shard_map.102 = bf16[128,16,128]{2,1,0:T(8,128)(2,1)} custom-call(f32[16,128,256]{2,1,0:T(8,128)S(1)} %copy-done.2, f32[16,128,128]{2,1,0:T(8,128)S(1)} %shard_map.101.s_ref, bf16[128,16,128]{2,1,0:T(8,128)(2,1)S(1)} %bitcast.26, f32[16,128]{1,0:T(8,128)S(1)} %copy-done.11), custom_call_target="tpu_custom_call" | custom-call | tf_op jit(solution)/shard_map/pallas_call | solution.py:322
  (1 shorter events, 0.0 us)
Async XLA Ops:
  0.0 4.1 %copy-start = (f32[1,128,16]{1,2,0:T(8,128)S(1)}, f32[1,128,16]{1,2,0:T(8,128)}, u32[]{:S(2)}) copy-start(f32[1,128,16]{1,2,0:T(8,128)} %param.14) | copy-start | bytes 24580
  2.8 6.8 %collective-permute-start = (bf16[1,3,5,16,128]{4,3,2,1,0:T(8,128)(2,1)}, bf16[1,3,5,16,128]{4,3,2,1,0:T(8,128)(2,1)}, u32[]{:S(2)}, u32[]{:S(2)}) collective-permute-start(bf16[1,3,5,16,128]{4,3,2,1,0:T(8,128)(2,1)} %pad_maximum_fusion), channel_id=1, source_target_pairs={{0,2},{2,4},{4,6},{6,8},{8,10},{10,12},{12,14},{14,16},{16,18},{18... | collective-permute-start | bytes 184328 | tf_op jit(solution)/shard_map/ppermute | solution.py:350
  5.3 5.9 %copy-start.3 = (bf16[1,128,2,16,128]{4,3,2,1,0:T(8,128)(2,1)S(1)}, bf16[1,128,2,16,128]{4,3,2,1,0:T(8,128)(2,1)}, u32[]{:S(2)}) copy-start(bf16[1,128,2,16,128]{4,3,2,1,0:T(8,128)(2,1)} %param.11) | copy-start | bytes 3145732
  5.3 5.9 %copy-start.4 = (bf16[1,128,2,16,128]{4,3,2,1,0:T(8,128)(2,1)S(1)}, bf16[1,128,2,16,128]{4,3,2,1,0:T(8,128)(2,1)}, u32[]{:S(2)}) copy-start(bf16[1,128,2,16,128]{4,3,2,1,0:T(8,128)(2,1)} %param.12) | copy-start | bytes 3145732
  5.3 5.9 %copy-start.7 = (f32[4,2,16,128]{3,2,1,0:T(8,128)S(1)}, f32[4,2,16,128]{3,2,1,0:T(8,128)}, u32[]{:S(2)}) copy-start(f32[4,2,16,128]{3,2,1,0:T(8,128)} %fk_ref.1) | copy-start | bytes 196612
  5.3 5.9 %copy-start.8 = (f32[4,2,16,128]{3,2,1,0:T(8,128)S(1)}, f32[4,2,16,128]{3,2,1,0:T(8,128)}, u32[]{:S(2)}) copy-start(f32[4,2,16,128]{3,2,1,0:T(8,128)} %fv_ref.1) | copy-start | bytes 196612
  11.2 1.0 %copy-start.5 = (bf16[1,128,16,128]{3,2,1,0:T(8,128)(2,1)S(1)}, bf16[1,128,16,128]{3,2,1,0:T(8,128)(2,1)}, u32[]{:S(2)}) copy-start(bf16[1,128,16,128]{3,2,1,0:T(8,128)(2,1)} %param.10) | copy-start | bytes 1572868
  12.2 0.7 copy-start.9
  12.9 0.8 copy-start.10
  47.9 1.6 %copy-start.1 = (f32[16,128,256]{2,1,0:T(8,128)S(1)}, f32[16,128,256]{2,1,0:T(8,128)}, u32[]{:S(2)}) copy-start(f32[16,128,256]{2,1,0:T(8,128)} %get-tuple-element.8.ab_ref) | copy-start | bytes 6291460
  49.5 43.1 %copy-start.2 = (f32[16,128,256]{2,1,0:T(8,128)S(1)}, f32[16,128,256]{2,1,0:T(8,128)}, u32[]{:S(2)}) copy-start(f32[16,128,256]{2,1,0:T(8,128)} %get-tuple-element.7.pb_ref) | copy-start | bytes 6291460
  49.5 43.1 %copy-start.6 = (bf16[1,128,16,128]{3,2,1,0:T(8,128)(2,1)S(1)}, bf16[1,128,16,128]{3,2,1,0:T(8,128)(2,1)}, u32[]{:S(2)}) copy-start(bf16[1,128,16,128]{3,2,1,0:T(8,128)(2,1)} %param.15) | copy-start | bytes 1572868
  49.5 43.1 %copy-start.11 = (f32[16,128]{1,0:T(8,128)S(1)}, f32[16,128]{1,0:T(8,128)}, u32[]{:S(2)}) copy-start(f32[16,128]{1,0:T(8,128)} %gain_ref.1) | copy-start | bytes 24580

commit v2 on v1

--- a/solution.py
+++ b/solution.py
@@ -1,5 +1,3 @@
-import functools
-
 import jax
 import jax.numpy as jnp
 from jax import lax
@@ -28,6 +26,10 @@
     return lax.dot_general(a, b, (((1,), (1,)), ((), ())), preferred_element_type=F32)
 
 
+def exact(a, b):
+    return jnp.dot(a, b, precision=HIGH, preferred_element_type=F32)
+
+
 def pair(x):
     return jnp.concatenate(split(x), 1)
 
@@ -52,7 +54,7 @@
     return dot(left_hi, hi) + (dot(left_lo, hi) + dot(left_hi, lo))
 
 
-def conv_into(x_ref, rim_ref, filter_ref, buf, normalize):
+def conv_into(x_ref, rim_value, filter_ref, buf, normalize):
     taps = filter_ref.shape[0]
     rim = taps - 1
     tok = x_ref.shape[0]
@@ -68,7 +70,7 @@
         buf[pl.ds(start, rows), :] = out.reshape(rows, out.shape[-1])
 
     finish(
-        jnp.concatenate([rim_ref[...].astype(F32), x_ref[0:CHUNK].astype(F32)], 0), 0
+        jnp.concatenate([rim_value.astype(F32), x_ref[0:CHUNK].astype(F32)], 0), 0
     )
 
     @pl.loop(1, tok // CHUNK)
@@ -78,9 +80,8 @@
 
 
 def local_kernel(
-    q_ref, k_ref, v_ref, rq_ref, rk_ref, rv_ref, fq_ref, fk_ref, fv_ref,
-    cum_ref, rate_ref, tok_ref, row_ref,
-    pb_ref, ab_ref, q_buf, k_buf, v_buf,
+    q_ref, k_ref, v_ref, rim_ref, fq_ref, fk_ref, fv_ref, decay_ref, rate_ref,
+    pb_ref, ab_ref, q_buf, k_buf, v_buf, cum_buf, rate_buf, tok_buf,
 ):
     heads = q_ref.shape[1]
     tok = q_ref.shape[0]
@@ -90,9 +91,41 @@
 
     @pl.when(pl.program_id(0) == 0)
     def _():
-        conv_into(q_ref, rq_ref, fq_ref, q_buf, True)
-        conv_into(k_ref, rk_ref, fk_ref, k_buf, True)
-        conv_into(v_ref, rv_ref, fv_ref, v_buf, False)
+        conv_into(q_ref, rim_ref[:, 0], fq_ref, q_buf, True)
+        conv_into(k_ref, rim_ref[:, 1 : 1 + refl], fk_ref, k_buf, True)
+        conv_into(v_ref, rim_ref[:, 1 + refl :], fv_ref, v_buf, False)
+        step = lax.broadcasted_iota(jnp.int32, (steps, tok), 0)
+        token = lax.broadcasted_iota(jnp.int32, (steps, tok), 1)
+        decay = decay_ref[...]
+        cum_buf[...] = exact(jnp.where(token * refl <= step, 1.0, 0.0), decay)
+        trow = lax.broadcasted_iota(jnp.int32, (tok, tok), 0)
+        tcol = lax.broadcasted_iota(jnp.int32, (tok, tok), 1)
+        tok_buf[...] = exact(jnp.where(tcol <= trow, 1.0, 0.0), decay)
+        rate_buf[...] = sum(
+            exact(jnp.where(token * refl + j == step, 1.0, 0.0), rate_ref[:, j])
+            for j in range(refl)
+        )
+
+    here = pl.program_id(0) * group
+    pick = jnp.where(
+        lax.broadcasted_iota(jnp.int32, (heads, 128), 0)
+        == here + lax.broadcasted_iota(jnp.int32, (heads, 128), 1),
+        1.0,
+        0.0,
+    )
+    pick_rows = jnp.where(
+        here + lax.broadcasted_iota(jnp.int32, (8, heads), 0)
+        == lax.broadcasted_iota(jnp.int32, (8, heads), 1),
+        1.0,
+        0.0,
+    )
+    cums = exact(cum_buf[...], pick)
+    rates = exact(rate_buf[...], pick)
+    toks = exact(tok_buf[...], pick)
+    cum_rows = lax.dot_general(
+        pick_rows, cum_buf[...], (((1,), (1,)), ((), ())), precision=HIGH,
+        preferred_element_type=F32,
+    )
 
     half = steps // 2
     row = lax.broadcasted_iota(jnp.int32, (half, half), 0)
@@ -110,10 +143,10 @@
         K = k_buf[pl.ds(head, steps, stride=heads), :]
         V = v_buf[pl.ds(head, steps, stride=heads), :]
         Q = q_buf[pl.ds(head, tok, stride=heads), :]
-        cum = cum_ref[0, :, g : g + 1]
-        rate = rate_ref[0, :, g : g + 1]
-        cum_tok = tok_ref[0, :, g : g + 1]
-        cum_row = row_ref[0, g : g + 1, :]
+        cum = cums[:, g : g + 1]
+        rate = rates[:, g : g + 1]
+        cum_tok = toks[:, g : g + 1]
+        cum_row = cum_rows[g : g + 1, :]
         last = cum_row[:, steps - 1 : steps]
         k_hi, k_lo = split(K)
         q_hi, q_lo = split(Q)
@@ -169,70 +202,114 @@
         solved = jnp.concatenate([top, bottom], 0)
         ab = mm_deep(keys_t, solved)
         pb = mm_deep(mixing, solved)
-        ab_ref[g, :, :dim] = jnp.where(drow == dcol, jnp.exp(-last), 0.0) - ab[:, :dim]
-        ab_ref[g, :, dim:] = ab[:, dim:]
+        ab_ref[g, :dim] = jnp.where(drow == dcol, jnp.exp(-last), 0.0) - ab[:, :dim].T
+        ab_ref[g, dim:] = ab[:, dim:].T
         pb_ref[g, :, :dim] = jnp.exp(-cum_tok) * Q - pb[:, :dim]
         pb_ref[g, :, dim:] = pb[:, dim:]
 
 
-def chain_kernel(ab_ref, s_ref, recv, send, send_sem, recv_sem):
+def chain_kernel(
+    ab_ref, s_ref, other, recv, send, back, mine,
+    ex_send, ex_recv, st_send, st_recv, rt_send, rt_recv,
+):
     count = lax.axis_size("seq")
     me = lax.axis_index("seq")
-    right = lax.rem(me + 1, count)
-    left = lax.rem(me + count - 1, count)
-    heads, dim = ab_ref.shape[0], ab_ref.shape[1]
+    side = lax.rem(me, 2)
+    place = lax.div(me, 2)
+    places = count // 2
+    partner = me + 1 - 2 * side
+    ahead = lax.rem(me + 2, count)
+    behind = lax.rem(me + count - 2, count)
+    heads, dim = ab_ref.shape[0], ab_ref.shape[2]
+    half = heads // 2
+    first = side * half
     barrier = pltpu.get_barrier_semaphore()
 
-    @pl.when(me > 0)
+    def signal(device):
+        pl.semaphore_signal(
+            barrier, inc=1, device_id={"seq": device}, device_id_type=pl.DeviceIdType.MESH
+        )
+
+    signal(partner)
+
+    @pl.when(place > 0)
     def _():
-        pl.semaphore_signal(
-            barrier, inc=1, device_id={"seq": left}, device_id_type=pl.DeviceIdType.MESH
+        signal(behind)
+
+    @pl.when(place < places - 1)
+    def _():
+        signal(ahead)
+
+    pl.semaphore_wait(
+        barrier, 1 + jnp.minimum(place, 1) + jnp.minimum(places - 1 - place, 1)
+    )
+
+    def remote(src, dst, send_sem, recv_sem, device):
+        return pltpu.make_async_remote_copy(
+            src_ref=src, dst_ref=dst, send_sem=send_sem, recv_sem=recv_sem,
+            device_id={"seq": device}, device_id_type=pl.DeviceIdType.MESH,
         )
 
-    @pl.when(me < count - 1)
-    def _():
-        pl.semaphore_signal(
-            barrier, inc=1, device_id={"seq": right}, device_id_type=pl.DeviceIdType.MESH
+    def exchange(i):
+        return remote(
+            ab_ref.at[half - first + i], other.at[i], ex_send.at[i], ex_recv.at[i], partner
         )
 
-    pl.semaphore_wait(barrier, jnp.minimum(me, 1) + jnp.minimum(count - 1 - me, 1))
-
-    def copy(h):
-        return pltpu.make_async_remote_copy(
-            src_ref=send.at[h],
-            dst_ref=recv.at[h],
-            send_sem=send_sem.at[h],
-            recv_sem=recv_sem.at[h],
-            device_id={"seq": right},
-            device_id_type=pl.DeviceIdType.MESH,
-        )
-
-    @pl.when(me == 0)
+    def onward(i):
+        return remote(send.at[i], recv.at[i], st_send.at[i], st_recv.at[i], ahead)
+
+    def hand_back(i):
+        return remote(back.at[i], mine.at[i], rt_send.at[i], rt_recv.at[i], partner)
+
+    @pl.loop(0, half)
+    def _(i):
+        exchange(i).start()
+
+    @pl.when(place == 0)
     def _():
         recv[...] = jnp.zeros_like(recv)
 
-    @pl.loop(0, heads)
-    def _(h):
-        left_pair = pair(ab_ref[h, :, :dim])
-
-        @pl.when(me > 0)
+    @pl.loop(0, half)
+    def _(i):
+        exchange(i).wait_recv()
+        own_map, other_map = ab_ref[first + i], other[i]
+        early = jnp.where(side == 0, own_map, other_map)
+        late = jnp.where(side == 0, other_map, own_map)
+        joined = mm_square(pair(early), late[:dim])
+        joined_b = joined[dim:] + late[dim:]
+
+        @pl.when(place > 0)
         def _():
-            copy(h).wait_recv()
-
-        state = recv[h]
-
-        @pl.when(me < count - 1)
+            onward(i).wait_recv()
+
+        state = recv[i]
+        state_pair = pair(state)
+
+        @pl.when(place < places - 1)
         def _():
-            send[h] = mm_square(left_pair, state) + ab_ref[h, :, dim:]
-            copy(h).start()
-
-        s_ref[h] = state
-
-    @pl.when(me < count - 1)
+            send[i] = mm_square(state_pair, joined[:dim]) + joined_b
+            onward(i).start()
+
+        later = mm_square(state_pair, early[:dim]) + early[dim:]
+        s_ref[first + i] = jnp.where(side == 0, state, later)
+        back[i] = jnp.where(side == 0, later, state)
+        hand_back(i).start()
+
+    @pl.loop(0, half)
+    def _(i):
+        hand_back(i).wait_recv()
+        s_ref[half - first + i] = mine[i]
+
+    @pl.loop(0, half)
+    def _(i):
+        exchange(i).wait_send()
+        hand_back(i).wait_send()
+
+    @pl.when(place < places - 1)
     def _():
-        @pl.loop(0, heads)
-        def _(h):
-            copy(h).wait_send()
+        @pl.loop(0, half)
+        def _(i):
+            onward(i).wait_send()
 
 
 def out_kernel(pb_ref, s_ref, gate_ref, gain_ref, out_ref, buf):
@@ -242,7 +319,7 @@
     def _(step):
         for g in range(GROUP):
             h = step * GROUP + g
-            value = mm_square(pair(pb_ref[h, :, :dim]), s_ref[h]) + pb_ref[h, :, dim:]
+            value = mm_square(pair(pb_ref[h, :, :dim]), s_ref[h].T) + pb_ref[h, :, dim:]
             buf[pl.ds(h, tok, stride=heads), :] = value
 
     rows = 8 * heads
@@ -264,43 +341,30 @@
     steps = tok * refl
     group = GROUP
     parts = heads // group
-    order = lax.broadcasted_iota(jnp.int32, (tok, tok), 0) >= lax.broadcasted_iota(
-        jnp.int32, (tok, tok), 1
-    )
-    cum = jnp.dot(order.astype(F32), decay, precision=HIGH)
-    cum_steps = jnp.repeat(cum, refl, axis=0)
-
-    def columns(x):
-        return x.reshape(x.shape[0], parts, group).transpose(1, 0, 2)
 
     def whole(shape):
         return pl.BlockSpec(shape, lambda i: (0,) * len(shape))
 
-    def part(shape):
-        return pl.BlockSpec((1,) + shape, lambda i: (i, 0, 0))
-
-    args = (
-        q, k, v, rims[:, 0], rims[:, 1 : 1 + refl], rims[:, 1 + refl :], fq, fk, fv,
-        columns(cum_steps), columns(rate.reshape(steps, heads)), columns(cum),
-        cum_steps.T.reshape(parts, group, steps),
-    )
+    args = (q, k, v, rims, fq, fk, fv, decay, rate)
     pb, ab = pl.pallas_call(
         local_kernel,
         grid=(parts,),
-        in_specs=[whole(x.shape) for x in args[:9]]
-        + [part((steps, group)), part((steps, group)), part((tok, group)), part((group, steps))],
+        in_specs=[whole(x.shape) for x in args],
         out_specs=[
             pl.BlockSpec((group, tok, 2 * dim), lambda i: (i, 0, 0)),
-            pl.BlockSpec((group, dim, 2 * dim), lambda i: (i, 0, 0)),
+            pl.BlockSpec((group, 2 * dim, dim), lambda i: (i, 0, 0)),
         ],
         out_shape=[
             jax.ShapeDtypeStruct((heads, tok, 2 * dim), F32),
-            jax.ShapeDtypeStruct((heads, dim, 2 * dim), F32),
+            jax.ShapeDtypeStruct((heads, 2 * dim, dim), F32),
         ],
         scratch_shapes=[
             pltpu.VMEM((tok * heads, dim), F32),
             pltpu.VMEM((steps * heads, dim), F32),
             pltpu.VMEM((steps * heads, dim), F32),
+            pltpu.VMEM((steps, heads), F32),
+            pltpu.VMEM((steps, heads), F32),
+            pltpu.VMEM((tok, heads), F32),
         ],
         compiler_params=pltpu.CompilerParams(vmem_limit_bytes=48 * 2**20),
     )(*args)
@@ -310,11 +374,10 @@
         out_specs=VMEM,
         out_shape=jax.ShapeDtypeStruct((heads, dim, dim), F32),
         scratch_shapes=[
-            pltpu.VMEM((heads, dim, dim), F32),
-            pltpu.VMEM((heads, dim, dim), F32),
-            pltpu.SemaphoreType.DMA((heads,)),
-            pltpu.SemaphoreType.DMA((heads,)),
-        ],
+            pltpu.VMEM((heads // 2, 2 * dim, dim), F32),
+        ]
+        + [pltpu.VMEM((heads // 2, dim, dim), F32)] * 4
+        + [pltpu.SemaphoreType.DMA((heads // 2,))] * 6,
         compiler_params=pltpu.CompilerParams(
             collective_id=0, has_side_effects=True, vmem_limit_bytes=32 * 2**20
         ),

time: 97.1 us -> 95.2 us (0.980)
  local copies, waits for them, and re-layouts: 13.2 us -> 11.3 us
    unnamed x25 -> x20, local copies, waits for them, and re-layouts: 4.98 us -> 9.16 us
    another operation x2 -> x0, local copies, waits for them, and re-layouts: 2.2 us -> none  [columns(): return x.reshape(x.shape[0], parts, group).transpose(1, 0, 2)]
    pallas_call x1, Pallas kernels: 34.2 us -> 36.3 us  [one_prompt(): pl.pallas_call(local_kernel, grid=(parts,), in_specs=[whole(x.shape) for...]
    pallas_call x1, Pallas kernels: 43 us -> 41.1 us  [one_prompt(): pl.pallas_call(chain_kernel, in_specs=[VMEM], out_specs=VMEM, out_shape=j...]
    transpose x2 -> x0, local copies, waits for them, and re-layouts: 1.33 us -> none  [the longest x1 1.27 us: columns(): return x.reshape(x.shape[0], parts, group).transpose(1, 0, 2)]
  transfers between devices with their start and end apart: 1 -> 1, of which waited for: 0 -> 1; matrix products, arithmetic and copies ran while one was open for 6% -> 2% of each run, Pallas kernels for 0% -> 0%
where the time goes in v2:
time: 95.2 us; the launch traced here: 94.5 us
  Pallas kernels  81.5 us (86%)
  local copies, waits for them, and re-layouts  11.3 us (12%)
  starting transfers between devices  1.29 us (1%)
    pallas_call x1, Pallas kernels, one_prompt(): pl.pallas_call(chain_kernel, in_specs=[VMEM], out_specs=VMEM, out_shape=j...  41.1 us
    pallas_call x1, Pallas kernels, one_prompt(): pl.pallas_call(local_kernel, grid=(parts,), in_specs=[whole(x.shape) for...  36.3 us
    unnamed x20, local copies, waits for them, and re-layouts  9.16 us
    pallas_call x1, Pallas kernels, one_prompt(): pl.pallas_call(out_kernel, in_specs=[VMEM] * 4, out_specs=VMEM, out_shape...  4.09 us
  transfers between devices with their start and end apart: 1, of which 1 were waited for; matrix products, arithmetic and copies ran while one was open for 2% of the time, Pallas kernels for 0%

profile of v2, /device:TPU:29, one launch (start us, length us, event | category | flops | bytes accessed | tf_op | source)
XLA Modules:
  0.0 94.5 jit_solution(1424086822168552534)
XLA Ops:
  0.0 0.7 slice_bitcast_fusion
  0.7 0.7 slice.10
  1.4 0.7 slice.11
  2.2 1.3 %collective-permute-start = (bf16[1,3,5,16,128]{4,3,2,1,0:T(8,128)(2,1)S(1)}, bf16[1,3,5,16,128]{4,3,2,1,0:T(8,128)(2,1)S(1)}, u32[]{:S(2)}, u32[]{:S(2)}) collective-permute-start(bf16[1,3,5,16,128]{4,3,2,1,0:T(8,128)(2,1)S(1)} %pad_maximum_fusion), channel_id=1, source_target_pairs={{0,2},{2,4},{4,6},{6,8},{8,10},{10,12},{12,14},{14,16},{16,18},{18... | collective-permute-start | bytes 184328 | tf_op jit(solution)/shard_map/ppermute | solution.py:413
  3.5 0.8 copy.11
  4.3 0.8 copy.12
  5.1 0.4 collective-permute-done
  5.5 0.0 copy-start.1
  5.5 1.2 %copy-done.1 = bf16[1,128,2,16,128]{4,3,2,1,0:T(8,128)(2,1)S(1)} copy-done((bf16[1,128,2,16,128]{4,3,2,1,0:T(8,128)(2,1)S(1)}, bf16[1,128,2,16,128]{4,3,2,1,0:T(8,128)(2,1)}, u32[]{:S(2)}) %copy-start.1) | copy-done | bytes 1048600
  6.7 0.0 copy-start.2
  6.7 1.2 %copy-done.2 = bf16[1,128,2,16,128]{4,3,2,1,0:T(8,128)(2,1)S(1)} copy-done((bf16[1,128,2,16,128]{4,3,2,1,0:T(8,128)(2,1)S(1)}, bf16[1,128,2,16,128]{4,3,2,1,0:T(8,128)(2,1)}, u32[]{:S(2)}) %copy-start.2) | copy-done | bytes 1048600
  8.0 0.0 copy-start.3
  8.0 1.0 %copy-done.3 = bf16[1,128,16,128]{3,2,1,0:T(8,128)(2,1)S(1)} copy-done((bf16[1,128,16,128]{3,2,1,0:T(8,128)(2,1)S(1)}, bf16[1,128,16,128]{3,2,1,0:T(8,128)(2,1)}, u32[]{:S(2)}) %copy-start.3) | copy-done | bytes 524312
  9.0 0.0 copy-start.5
  9.0 0.8 copy-done.5
  9.9 0.0 copy-start.6
  9.9 0.8 copy-done.6
  10.7 0.0 copy-start.7
  10.7 0.8 copy-done.7
  11.5 36.3 %shard_map.100 = (f32[16,128,256]{2,1,0:T(8,128)S(1)}, f32[16,256,128]{2,1,0:T(8,128)}) custom-call(bf16[128,16,128]{2,1,0:T(8,128)(2,1)S(1)} %bitcast.12, bf16[128,2,16,128]{3,2,1,0:T(8,128)(2,1)S(1)} %bitcast.10, bf16[128,2,16,128]{3,2,1,0:T(8,128)(2,1)S(1)} %bitcast.11, bf16[3,5,16,128]{3,2,1,0:T(8,128)(2,1)S(1)} %bitcast.16, ...), custom_call_target="tpu_custom_call" | custom-call | tf_op jit(solution)/shard_map/pallas_call | solution.py:349
  47.8 0.0 copy-start
  47.8 1.6 %copy-done = f32[16,256,128]{2,1,0:T(8,128)S(1)} copy-done((f32[16,256,128]{2,1,0:T(8,128)S(1)}, f32[16,256,128]{2,1,0:T(8,128)}, u32[]{:S(2)}) %copy-start) | copy-done | bytes 2097176
  49.4 0.0 copy-start.4
  49.4 0.0 copy-start.8
  49.4 41.1 %shard_map.101.s_ref = f32[16,128,128]{2,1,0:T(8,128)S(1)} custom-call(f32[16,256,128]{2,1,0:T(8,128)S(1)} %copy-done), custom_call_target="tpu_custom_call" | custom-call | tf_op jit(solution)/shard_map/pallas_call | solution.py:371
  90.4 0.0 copy-done.4
  90.4 0.0 copy-done.8
  90.4 4.1 %shard_map.102 = bf16[128,16,128]{2,1,0:T(8,128)(2,1)} custom-call(f32[16,128,256]{2,1,0:T(8,128)S(1)} %get-tuple-element.7.pb_ref, f32[16,128,128]{2,1,0:T(8,128)S(1)} %shard_map.101.s_ref, bf16[128,16,128]{2,1,0:T(8,128)(2,1)S(1)} %bitcast.14, f32[16,128]{1,0:T(8,128)S(1)} %copy-done.8), custom_call_target="tpu_custom_call" | custom-call | tf_op jit(solution)/shard_map/pallas_call | solution.py:385
  (1 shorter events, 0.0 us)
Async XLA Ops:
  2.2 3.3 %collective-permute-start = (bf16[1,3,5,16,128]{4,3,2,1,0:T(8,128)(2,1)S(1)}, bf16[1,3,5,16,128]{4,3,2,1,0:T(8,128)(2,1)S(1)}, u32[]{:S(2)}, u32[]{:S(2)}) collective-permute-start(bf16[1,3,5,16,128]{4,3,2,1,0:T(8,128)(2,1)S(1)} %pad_maximum_fusion), channel_id=1, source_target_pairs={{0,2},{2,4},{4,6},{6,8},{8,10},{10,12},{12,14},{14,16},{16,18},{18... | collective-permute-start | bytes 184328 | tf_op jit(solution)/shard_map/ppermute | solution.py:413
  5.5 1.2 %copy-start.1 = (bf16[1,128,2,16,128]{4,3,2,1,0:T(8,128)(2,1)S(1)}, bf16[1,128,2,16,128]{4,3,2,1,0:T(8,128)(2,1)}, u32[]{:S(2)}) copy-start(bf16[1,128,2,16,128]{4,3,2,1,0:T(8,128)(2,1)} %param.11) | copy-start | bytes 3145732
  6.7 1.2 %copy-start.2 = (bf16[1,128,2,16,128]{4,3,2,1,0:T(8,128)(2,1)S(1)}, bf16[1,128,2,16,128]{4,3,2,1,0:T(8,128)(2,1)}, u32[]{:S(2)}) copy-start(bf16[1,128,2,16,128]{4,3,2,1,0:T(8,128)(2,1)} %param.12) | copy-start | bytes 3145732
  8.0 1.0 %copy-start.3 = (bf16[1,128,16,128]{3,2,1,0:T(8,128)(2,1)S(1)}, bf16[1,128,16,128]{3,2,1,0:T(8,128)(2,1)}, u32[]{:S(2)}) copy-start(bf16[1,128,16,128]{3,2,1,0:T(8,128)(2,1)} %param.10) | copy-start | bytes 1572868
  9.0 0.8 copy-start.5
  9.9 0.8 copy-start.6
  10.7 0.8 copy-start.7
  47.8 1.6 %copy-start = (f32[16,256,128]{2,1,0:T(8,128)S(1)}, f32[16,256,128]{2,1,0:T(8,128)}, u32[]{:S(2)}) copy-start(f32[16,256,128]{2,1,0:T(8,128)} %get-tuple-element.8.ab_ref) | copy-start | bytes 6291460
  49.4 41.1 %copy-start.4 = (bf16[1,128,16,128]{3,2,1,0:T(8,128)(2,1)S(1)}, bf16[1,128,16,128]{3,2,1,0:T(8,128)(2,1)}, u32[]{:S(2)}) copy-start(bf16[1,128,16,128]{3,2,1,0:T(8,128)(2,1)} %param.15) | copy-start | bytes 1572868
  49.4 41.1 %copy-start.8 = (f32[16,128]{1,0:T(8,128)S(1)}, f32[16,128]{1,0:T(8,128)}, u32[]{:S(2)}) copy-start(f32[16,128]{1,0:T(8,128)} %gain_ref.1) | copy-start | bytes 24580

commit v3 on v1

v3 whole, which is shorter than its diff:
```python
import jax
import jax.numpy as jnp
from jax import lax
from jax.experimental import pallas as pl
from jax.experimental.pallas import tpu as pltpu
from jax.sharding import PartitionSpec as P

HIGH = lax.Precision.HIGHEST
epsilon = 1e-06
CHUNK = 4
GROUP = 4
PIECES = 2
F32 = jnp.float32
BF16 = jnp.bfloat16


def split(x):
    hi = x.astype(BF16)
    return hi, (x - hi.astype(F32)).astype(BF16)


def dot(a, b):
    return jnp.dot(a, b, preferred_element_type=F32)


def dot_nt(a, b):
    return lax.dot_general(a, b, (((1,), (1,)), ((), ())), preferred_element_type=F32)


def exact(a, b):
    return jnp.dot(a, b, precision=HIGH, preferred_element_type=F32)


def pair(x):
    return jnp.concatenate(split(x), 1)


def mm_square(left_pair, right):
    rows = pair(right)
    out = dot(left_pair, jnp.concatenate([rows, rows], 0))
    width = right.shape[1]
    return out[:, :width] + out[:, width:]


def mm_wide(left, right):
    left_hi, left_lo = split(left)
    hi, lo = split(right)
    both = jnp.concatenate([left_hi, left_lo], 1)
    return dot(both, jnp.concatenate([hi, hi], 0)) + dot(left_hi, lo)


def mm_deep(left, right):
    left_hi, left_lo = split(left)
    hi, lo = split(right)
    return dot(left_hi, hi) + (dot(left_lo, hi) + dot(left_hi, lo))


def conv_into(x_ref, rim_ref, filter_ref, buf, normalize, edge):
    taps = filter_ref.shape[0]
    rim = taps - 1
    tok = x_ref.shape[0]
    rows = CHUNK * (buf.shape[0] // tok)

    def finish(window, start):
        summed = jnp.zeros((CHUNK,) + window.shape[1:], F32)
        for tap in range(taps):
            summed = summed + filter_ref[tap] * window[tap : tap + CHUNK]
        out = jax.nn.silu(summed)
        if normalize:
            out = out / jnp.sqrt(jnp.sum(out * out, -1, keepdims=True) + epsilon)
        buf[pl.ds(start, rows), :] = out.reshape(rows, out.shape[-1])

    if edge:
        finish(
            jnp.concatenate([rim_ref[...].astype(F32), x_ref[0:CHUNK].astype(F32)], 0), 0
        )
        return

    @pl.loop(1, tok // CHUNK)
    def _(step):
        window = x_ref[pl.ds(step * CHUNK - rim, CHUNK + rim)].astype(F32)
        finish(window, pl.multiple_of(step * rows, rows))


def shard_kernel(
    q_ref, k_ref, v_ref, fq_ref, fk_ref, fv_ref, decay_ref, rate_ref,
    pb_ref, s_ref,
    q_buf, k_buf, v_buf, cum_buf, rate_buf, tok_buf, rim_q, rim_k, rim_v,
    maps, other, recv, send, back, mine,
    rim_send, rim_recv, ex_send, ex_recv, st_send, st_recv, rt_send, rt_recv,
):
    heads, tok, refl, dim = q_ref.shape[1], q_ref.shape[0], k_ref.shape[1], q_ref.shape[2]
    steps = tok * refl
    group = pb_ref.shape[0]
    own = group // 2
    parts = heads // group
    rim = rim_q.shape[0]
    turn = pl.program_id(0)

    count = lax.axis_size("seq")
    me = lax.axis_index("seq")
    side = lax.rem(me, 2)
    place = lax.div(me, 2)
    places = count // 2
    partner = me + 1 - 2 * side
    first = side * own
    rest = own - first

    def remote(src, dst, send_sem, recv_sem, device):
        return pltpu.make_async_remote_copy(
            src_ref=src, dst_ref=dst, send_sem=send_sem, recv_sem=recv_sem,
            device_id={"seq": device}, device_id_type=pl.DeviceIdType.MESH,
        )

    def rim_copies():
        ends = ((q_ref, rim_q), (k_ref, rim_k), (v_ref, rim_v))
        return [
            remote(
                src.at[pl.ds(tok - rim, rim)], dst, rim_send.at[n], rim_recv.at[n],
                lax.rem(me + 1, count),
            )
            for n, (src, dst) in enumerate(ends)
        ]

    def exchange(g, j):
        slot = g * own + j
        return remote(
            maps.at[g * group + rest + j], other.at[slot],
            ex_send.at[slot], ex_recv.at[slot], partner,
        )

    def onward(g, j, piece):
        slot = (g * own + j) * PIECES + piece
        return remote(
            send.at[slot], recv.at[slot], st_send.at[slot], st_recv.at[slot],
            lax.rem(me + 2, count),
        )

    def hand_back(g, j):
        slot = g * own + j
        return remote(back.at[slot], mine.at[slot], rt_send.at[slot], rt_recv.at[slot], partner)

    @pl.when(turn == 0)
    def _():
        barrier = pltpu.get_barrier_semaphore()
        for shift in (-2, -1, 1, 2):

            @pl.when((me + shift >= 0) & (me + shift < count))
            def _():
                pl.semaphore_signal(
                    barrier, inc=1, device_id={"seq": lax.rem(me + shift + count, count)},
                    device_id_type=pl.DeviceIdType.MESH,
                )

        pl.semaphore_wait(barrier, jnp.minimum(me, 2) + jnp.minimum(count - 1 - me, 2))

        @pl.when(me < count - 1)
        def _():
            for one in rim_copies():
                one.start()

        @pl.when(me == 0)
        def _():
            for one in (rim_q, rim_k, rim_v):
                one[...] = jnp.zeros_like(one)

        @pl.when(place == 0)
        def _():
            recv[...] = jnp.zeros_like(recv)

        def convs(edge):
            conv_into(q_ref, rim_q, fq_ref, q_buf, True, edge)
            conv_into(k_ref, rim_k, fk_ref, k_buf, True, edge)
            conv_into(v_ref, rim_v, fv_ref, v_buf, False, edge)

        convs(False)
        step = lax.broadcasted_iota(jnp.int32, (steps, tok), 0)
        token = lax.broadcasted_iota(jnp.int32, (steps, tok), 1)
        decay = decay_ref[...]
        cum_buf[...] = exact(jnp.where(token * refl <= step, 1.0, 0.0), decay)
        trow = lax.broadcasted_iota(jnp.int32, (tok, tok), 0)
        tcol = lax.broadcasted_iota(jnp.int32, (tok, tok), 1)
        tok_buf[...] = exact(jnp.where(tcol <= trow, 1.0, 0.0), decay)
        rate_buf[...] = sum(
            exact(jnp.where(token * refl + j == step, 1.0, 0.0), rate_ref[:, j])
            for j in range(refl)
        )

        @pl.when(me > 0)
        def _():
            for one in rim_copies():
                one.wait_recv()

        convs(True)

        @pl.when(me < count - 1)
        def _():
            for one in rim_copies():
                one.wait_send()

    @pl.when(turn < parts)
    def _():
        here = turn * group
        pick = jnp.where(
            lax.broadcasted_iota(jnp.int32, (heads, 128), 0)
            == here + lax.broadcasted_iota(jnp.int32, (heads, 128), 1),
            1.0,
            0.0,
        )
        pick_rows = jnp.where(
            here + lax.broadcasted_iota(jnp.int32, (8, heads), 0)
            == lax.broadcasted_iota(jnp.int32, (8, heads), 1),
            1.0,
            0.0,
        )
        cums = exact(cum_buf[...], pick)
        rates = exact(rate_buf[...], pick)
        toks = exact(tok_buf[...], pick)
        cum_rows = lax.dot_general(
            pick_rows, cum_buf[...], (((1,), (1,)), ((), ())), precision=HIGH,
            preferred_element_type=F32,
        )

        half = steps // 2
        row = lax.broadcasted_iota(jnp.int32, (half, half), 0)
        col = lax.broadcasted_iota(jnp.int32, (half, half), 1)
        qrow = lax.broadcasted_iota(jnp.int32, (tok, steps), 0)
        qcol = lax.broadcasted_iota(jnp.int32, (tok, steps), 1)
        eye = jnp.where(row == col, 1.0, 0.0)
        dim = q_ref.shape[2]
        drow = lax.broadcasted_iota(jnp.int32, (dim, dim), 0)
        dcol = lax.broadcasted_iota(jnp.int32, (dim, dim), 1)

        work = []
        for g in range(group):
            head = here + g
            K = k_buf[pl.ds(head, steps, stride=heads), :]
            V = v_buf[pl.ds(head, steps, stride=heads), :]
            Q = q_buf[pl.ds(head, tok, stride=heads), :]
            cum = cums[:, g : g + 1]
            rate = rates[:, g : g + 1]
            cum_tok = toks[:, g : g + 1]
            cum_row = cum_rows[g : g + 1, :]
            last = cum_row[:, steps - 1 : steps]
            k_hi, k_lo = split(K)
            q_hi, q_lo = split(Q)
            hi = jnp.concatenate([k_hi, q_hi], 0)
            lo = jnp.concatenate([k_lo, q_lo], 0)
            gram = dot_nt(
                jnp.concatenate([hi, lo], 1), jnp.concatenate([k_hi, k_hi], 1)
            ) + dot_nt(hi, k_lo)

            def lower(r, c):
                ratio = jnp.exp(
                    jnp.minimum(cum_row[:, c * half : (c + 1) * half] - cum[r * half : (r + 1) * half], 0.0)
                )
                block = gram[r * half : (r + 1) * half, c * half : (c + 1) * half]
                value = rate[r * half : (r + 1) * half] * ratio * block
                return jnp.where(row > col, value, 0.0) if r == c else value

            low = [lower(0, 0), lower(1, 1)]
            low_21 = lower(1, 0)
            mixing = jnp.where(
                qrow * refl + (refl - 1) >= qcol,
                gram[steps:] * jnp.exp(jnp.minimum(cum_row - cum_tok, 0.0)),
                0.0,
            )
            right = jnp.concatenate([(rate * jnp.exp(-cum)) * K, rate * V], 1)
            keys_t = K.T * jnp.exp(cum_row - last)
            work.append((low, low_21, mixing, right, keys_t, Q, cum_tok, last))

        inverse = [
            [eye - jnp.where((row // 2) == (col // 2), low, 0.0) for low in item[0]] for item in work
        ]
        size = 2
        while size < half:
            mask = ((row // (2 * size)) == (col // (2 * size))) & ((row // size) != (col // size))
            lefts = [[pair(x) for x in two] for two in inverse]
            inner = [
                [
                    mm_square(pair(jnp.where(mask, low, 0.0)), x)
                    for low, x in zip(item[0], two)
                ]
                for item, two in zip(work, inverse)
            ]
            inverse = [
                [x - mm_square(l, y) for x, l, y in zip(two, ls, ys)]
                for two, ls, ys in zip(inverse, lefts, inner)
            ]
            size *= 2

        for g, (item, two) in enumerate(zip(work, inverse)):
            low, low_21, mixing, right, keys_t, Q, cum_tok, last = item
            top = mm_wide(two[0], right[:half])
            bottom = mm_wide(two[1], right[half:] - mm_wide(low_21, top))
            solved = jnp.concatenate([top, bottom], 0)
            ab = mm_deep(keys_t, solved)
            pb = mm_deep(mixing, solved)
            maps[here + g, :dim] = jnp.where(drow == dcol, jnp.exp(-last), 0.0) - ab[:, :dim].T
            maps[here + g, dim:] = ab[:, dim:].T
            pb_ref[g, :, :dim] = jnp.exp(-cum_tok) * Q - pb[:, :dim]
            pb_ref[g, :, dim:] = pb[:, dim:]

        for j in range(own):
            exchange(turn, j).start()

    @pl.when(turn > 0)
    def _():
        g = turn - 1
        joins = []
        for j in range(own):
            exchange(g, j).wait_recv()
            own_map, other_map = maps[g * group + first + j], other[g * own + j]
            early = jnp.where(side == 0, own_map, other_map)
            late = jnp.where(side == 0, other_map, own_map)
            joined = mm_square(pair(early), late[:dim])
            joins.append((joined[:dim], joined[dim:] + late[dim:], early))
        rows = dim // PIECES
        for j in range(own):
            for piece in range(PIECES):

                @pl.when(place > 0)
                def _():
                    onward(g, j, piece).wait_recv()

                slot = (g * own + j) * PIECES + piece
                state_pair = pair(recv[slot])
                send[slot] = mm_square(state_pair, joins[j][0]) + joins[j][1][
                    piece * rows : (piece + 1) * rows
                ]

                @pl.when(place < places - 1)
                def _():
                    onward(g, j, piece).start()

        for j in range(own):
            slot = g * own + j
            state = jnp.concatenate([recv[slot * PIECES + piece] for piece in range(PIECES)], 0)
            early = joins[j][2]
            later = mm_square(pair(state), early[:dim]) + early[dim:]
            s_ref[g * group + first + j] = jnp.where(side == 0, state, later)
            back[slot] = jnp.where(side == 0, later, state)
            hand_back(g, j).start()

    @pl.when(turn == parts)
    def _():
        @pl.loop(0, parts)
        def _(g):
            for j in range(own):
                hand_back(g, j).wait_recv()
                s_ref[g * group + rest + j] = mine[g * own + j]
                exchange(g, j).wait_send()
                hand_back(g, j).wait_send()

        @pl.when(place < places - 1)
        def _():
            @pl.loop(0, parts)
            def _(g):
                for j in range(own):
                    for piece in range(PIECES):
                        onward(g, j, piece).wait_send()


def out_kernel(pb_ref, s_ref, gate_ref, gain_ref, out_ref, buf):
    heads, tok, dim = pb_ref.shape[0], pb_ref.shape[1], pb_ref.shape[2] // 2

    @pl.loop(0, heads // GROUP)
    def _(step):
        for g in range(GROUP):
            h = step * GROUP + g
            value = mm_square(pair(pb_ref[h, :, :dim]), s_ref[h].T) + pb_ref[h, :, dim:]
            buf[pl.ds(h, tok, stride=heads), :] = value

    rows = 8 * heads

    @pl.loop(0, tok // 8)
    def _(step):
        value = buf[pl.ds(pl.multiple_of(step * rows, rows), rows), :].reshape(8, heads, dim)
        normed = value / jnp.sqrt(jnp.mean(value * value, -1, keepdims=True) + epsilon)
        gate = jax.nn.silu(gate_ref[pl.ds(step * 8, 8)].astype(F32))
        out_ref[pl.ds(step * 8, 8)] = (normed * gain_ref[...] * gate).astype(out_ref.dtype)


VMEM = pl.BlockSpec(memory_space=pltpu.VMEM)


def one_prompt(q, k, v, rate, decay, gate, fq, fk, fv, gain):
    tok, heads, dim = q.shape
    refl = k.shape[1]
    steps = tok * refl
    group = GROUP
    parts = heads // group

    def whole(shape):
        return pl.BlockSpec(shape, lambda i: (0,) * len(shape))

    args = (q, k, v, fq, fk, fv, decay, rate)
    half = heads // 2
    rim = fq.shape[0] - 1
    dma = pltpu.SemaphoreType.DMA
    pb, states = pl.pallas_call(
        shard_kernel,
        grid=(parts + 1,),
        in_specs=[whole(x.shape) for x in args],
        out_specs=[
            pl.BlockSpec(
                (group, tok, 2 * dim), lambda i: (jnp.minimum(i, parts - 1), 0, 0)
            ),
            whole((heads, dim, dim)),
        ],
        out_shape=[
            jax.ShapeDtypeStruct((heads, tok, 2 * dim), F32),
            jax.ShapeDtypeStruct((heads, dim, dim), F32),
        ],
        scratch_shapes=[
            pltpu.VMEM((tok * heads, dim), F32),
            pltpu.VMEM((steps * heads, dim), F32),
            pltpu.VMEM((steps * heads, dim), F32),
            pltpu.VMEM((steps, heads), F32),
            pltpu.VMEM((steps, heads), F32),
            pltpu.VMEM((tok, heads), F32),
            pltpu.VMEM((rim, heads, dim), BF16),
            pltpu.VMEM((rim, refl, heads, dim), BF16),
            pltpu.VMEM((rim, refl, heads, dim), BF16),
            pltpu.VMEM((heads, 2 * dim, dim), F32),
            pltpu.VMEM((half, 2 * dim, dim), F32),
            pltpu.VMEM((half * PIECES, dim // PIECES, dim), F32),
            pltpu.VMEM((half * PIECES, dim // PIECES, dim), F32),
            pltpu.VMEM((half, dim, dim), F32),
            pltpu.VMEM((half, dim, dim), F32),
            dma((3,)), dma((3,)), dma((half,)), dma((half,)),
            dma((half * PIECES,)), dma((half * PIECES,)), dma((half,)), dma((half,)),
        ],
        compiler_params=pltpu.CompilerParams(
            collective_id=0, has_side_effects=True, vmem_limit_bytes=58 * 2**20
        ),
    )(*args)
    return pl.pallas_call(
        out_kernel,
        in_specs=[VMEM] * 4,
        out_specs=VMEM,
        out_shape=jax.ShapeDtypeStruct((tok, heads, dim), BF16),
        scratch_shapes=[pltpu.VMEM((tok * heads, dim), F32)],
        compiler_params=pltpu.CompilerParams(vmem_limit_bytes=32 * 2**20),
    )(pb, states, gate, gain)


def per_device(
    query_raw,
    key_raw,
    value_raw,
    write_rate,
    decay_rate,
    gate_input,
    filter_query,
    filter_key,
    filter_value,
    output_gain,
):
    return jnp.stack(
        [
            one_prompt(
                query_raw[p], key_raw[p], value_raw[p], write_rate[p], decay_rate[p],
                gate_input[p], filter_query, filter_key, filter_value, output_gain,
            )
            for p in range(query_raw.shape[0])
        ]
    )


def solution(mesh):
    return jax.shard_map(
        per_device,
        mesh=mesh,
        in_specs=(
            P(("grp", "prm"), "seq", "hd", None),
            P(("grp", "prm"), "seq", None, "hd", None),
            P(("grp", "prm"), "seq", None, "hd", None),
            P(("grp", "prm"), "seq", None, "hd"),
            P(("grp", "prm"), "seq", "hd"),
            P(("grp", "prm"), "seq", "hd", None),
            P(None, "hd", None),
            P(None, None, "hd", None),
            P(None, None, "hd", None),
            P("hd", None),
        ),
        out_specs=P(("grp", "prm"), "seq", "hd", None),
        check_vma=False,
    )
```

time: 97.1 us -> 84 us (0.87)
  local copies, waits for them, and re-layouts: 13.2 us -> 5.77 us
  Pallas kernels: 81 us -> 77.9 us
  starting transfers between devices: 1.28 us -> 0 us
    pallas_call x2 -> x1, Pallas kernels: 77.3 us -> 73.8 us  [one_prompt(): pl.pallas_call(shard_kernel, grid=(parts + 1,), in_specs=[whole(x.shape)...]
    slice x3 -> x0, local copies, waits for them, and re-layouts: 2.24 us -> none  [the longest x1 0.76 us: one_prompt(): rims[:, 1 + refl:]]
    another operation x2 -> x0, local copies, waits for them, and re-layouts: 2.2 us -> none  [columns(): return x.reshape(x.shape[0], parts, group).transpose(1, 0, 2)]
    transpose x2 -> x0, local copies, waits for them, and re-layouts: 1.33 us -> none  [the longest x1 1.27 us: columns(): return x.reshape(x.shape[0], parts, group).transpose(1, 0, 2)]
    ppermute x1 -> x0, starting transfers between devices: 1.28 us -> none  [per_device(): rims = lax.ppermute(edge, 'seq', [(i, i + 1) for i in range(count - 1)])]
    unnamed x25 -> x10, local copies, waits for them, and re-layouts: 4.98 us -> 5.77 us
  transfers between devices with their start and end apart: 1 -> 0, of which waited for: 0 -> 0; matrix products, arithmetic and copies ran while one was open for 6% -> 0% of each run, Pallas kernels for 0% -> 0%
where the time goes in v3:
time: 84 us; the launch traced here: 83.7 us
  Pallas kernels  77.9 us (93%)
  local copies, waits for them, and re-layouts  5.77 us (7%)
    pallas_call x1, Pallas kernels, one_prompt(): pl.pallas_call(shard_kernel, grid=(parts + 1,), in_specs=[whole(x.shape)...  73.8 us
    unnamed x10, local copies, waits for them, and re-layouts  5.77 us
    pallas_call x1, Pallas kernels, one_prompt(): pl.pallas_call(out_kernel, in_specs=[VMEM] * 4, out_specs=VMEM, out_shape...  4.08 us

profile of v3, /device:TPU:29, one launch (start us, length us, event | category | flops | bytes accessed | tf_op | source)
XLA Modules:
  0.0 83.7 jit_solution(9595777567400287284)
XLA Ops:
  0.0 0.0 copy-start.3
  0.0 0.0 copy-start.2
  0.0 1.5 %copy.11 = f32[1,128,16]{2,1,0:T(8,128)} copy(f32[1,128,16]{1,2,0:T(8,128)} %param.14) | data formatting | bytes 16384 | tf_op args[4]
  1.5 1.5 %copy.12 = f32[1,128,2,16]{3,2,1,0:T(2,128)} copy(f32[1,128,2,16]{1,3,2,0:T(8,128)} %param.13) | data formatting | bytes 32768 | tf_op args[3]
  3.0 73.8 %shard_map.100 = (f32[16,128,256]{2,1,0:T(8,128)}, f32[16,128,128]{2,1,0:T(8,128)}) custom-call(bf16[128,16,128]{2,1,0:T(8,128)(2,1)} %bitcast.11, bf16[128,2,16,128]{3,2,1,0:T(8,128)(2,1)} %bitcast.8, bf16[128,2,16,128]{3,2,1,0:T(8,128)(2,1)} %bitcast.9, f32[4,16,128]{2,1,0:T(8,128)} %fq_ref.1, f32[4,2,16,128]{3,2,1,0:T(8,128)} %fk_ref.1, ...), custom_call_target="tpu_custom_call" | custom-call | tf_op jit(solution)/shard_map/pallas_call | solution.py:401
  76.8 0.0 copy-done.3
  76.8 0.0 copy-done.2
  76.8 0.0 copy-start
  76.8 1.6 %copy-done = f32[16,128,256]{2,1,0:T(8,128)S(1)} copy-done((f32[16,128,256]{2,1,0:T(8,128)S(1)}, f32[16,128,256]{2,1,0:T(8,128)}, u32[]{:S(2)}) %copy-start) | copy-done | bytes 2097176
  78.4 0.0 copy-start.1
  78.4 1.2 %copy-done.1 = f32[16,128,128]{2,1,0:T(8,128)S(1)} copy-done((f32[16,128,128]{2,1,0:T(8,128)S(1)}, f32[16,128,128]{2,1,0:T(8,128)}, u32[]{:S(2)}) %copy-start.1) | copy-done | bytes 1048600
  79.6 4.1 %shard_map.101 = bf16[128,16,128]{2,1,0:T(8,128)(2,1)} custom-call(f32[16,128,256]{2,1,0:T(8,128)S(1)} %copy-done, f32[16,128,128]{2,1,0:T(8,128)S(1)} %copy-done.1, bf16[128,16,128]{2,1,0:T(8,128)(2,1)S(1)} %bitcast.7, f32[16,128]{1,0:T(8,128)S(1)} %copy-done.3), custom_call_target="tpu_custom_call" | custom-call | tf_op jit(solution)/shard_map/pallas_call | solution.py:438
Async XLA Ops:
  0.0 76.8 %copy-start.3 = (f32[16,128]{1,0:T(8,128)S(1)}, f32[16,128]{1,0:T(8,128)}, u32[]{:S(2)}) copy-start(f32[16,128]{1,0:T(8,128)} %gain_ref.1) | copy-start | bytes 24580
  0.0 76.8 %copy-start.2 = (bf16[1,128,16,128]{3,2,1,0:T(8,128)(2,1)S(1)}, bf16[1,128,16,128]{3,2,1,0:T(8,128)(2,1)}, u32[]{:S(2)}) copy-start(bf16[1,128,16,128]{3,2,1,0:T(8,128)(2,1)} %param.15) | copy-start | bytes 1572868
  76.8 1.6 %copy-start = (f32[16,128,256]{2,1,0:T(8,128)S(1)}, f32[16,128,256]{2,1,0:T(8,128)}, u32[]{:S(2)}) copy-start(f32[16,128,256]{2,1,0:T(8,128)} %get-tuple-element.7.pb_ref) | copy-start | bytes 6291460
  78.4 1.2 %copy-start.1 = (f32[16,128,128]{2,1,0:T(8,128)S(1)}, f32[16,128,128]{2,1,0:T(8,128)}, u32[]{:S(2)}) copy-start(f32[16,128,128]{2,1,0:T(8,128)} %get-tuple-element.8.s_ref) | copy-start | bytes 3145732

commit v4 on v3

--- a/solution.py
+++ b/solution.py
@@ -10,6 +10,7 @@
 CHUNK = 4
 GROUP = 4
 PIECES = 2
+SHARE = 4
 F32 = jnp.float32
 BF16 = jnp.bfloat16
 
@@ -29,6 +30,12 @@
 
 def exact(a, b):
     return jnp.dot(a, b, precision=HIGH, preferred_element_type=F32)
+
+
+def exact_nt(a, b):
+    return lax.dot_general(
+        a, b, (((1,), (1,)), ((), ())), precision=HIGH, preferred_element_type=F32
+    )
 
 
 def pair(x):
@@ -92,19 +99,18 @@
     heads, tok, refl, dim = q_ref.shape[1], q_ref.shape[0], k_ref.shape[1], q_ref.shape[2]
     steps = tok * refl
     group = pb_ref.shape[0]
-    own = group // 2
+    own = group // SHARE
     parts = heads // group
     rim = rim_q.shape[0]
     turn = pl.program_id(0)
 
     count = lax.axis_size("seq")
     me = lax.axis_index("seq")
-    side = lax.rem(me, 2)
-    place = lax.div(me, 2)
-    places = count // 2
-    partner = me + 1 - 2 * side
+    side = lax.rem(me, SHARE)
+    place = lax.div(me, SHARE)
+    places = count // SHARE
+    base = place * SHARE
     first = side * own
-    rest = own - first
 
     def remote(src, dst, send_sem, recv_sem, device):
         return pltpu.make_async_remote_copy(
@@ -122,37 +128,68 @@
             for n, (src, dst) in enumerate(ends)
         ]
 
-    def exchange(g, j):
+    def peer_side(d):
+        return lax.rem(side + d, SHARE)
+
+    def exchange(g, j, d, arriving=False):
         slot = g * own + j
+        peer = peer_side(d)
+        source = peer if arriving else side
         return remote(
-            maps.at[g * group + rest + j], other.at[slot],
-            ex_send.at[slot], ex_recv.at[slot], partner,
+            maps.at[g * group + peer * own + j], other.at[slot * SHARE + source],
+            ex_send.at[slot * SHARE + d], ex_recv.at[slot * SHARE + source], base + peer,
         )
 
     def onward(g, j, piece):
         slot = (g * own + j) * PIECES + piece
         return remote(
             send.at[slot], recv.at[slot], st_send.at[slot], st_recv.at[slot],
-            lax.rem(me + 2, count),
-        )
-
-    def hand_back(g, j):
+            lax.rem(me + SHARE, count),
+        )
+
+    def hand_back(g, j, d, arriving=False):
         slot = g * own + j
-        return remote(back.at[slot], mine.at[slot], rt_send.at[slot], rt_recv.at[slot], partner)
+        peer = peer_side(d)
+        head = g * group + (peer if arriving else side) * own + j
+        return remote(
+            back.at[slot * SHARE + peer], mine.at[head],
+            rt_send.at[slot * SHARE + d], rt_recv.at[head], base + peer,
+        )
 
     @pl.when(turn == 0)
     def _():
         barrier = pltpu.get_barrier_semaphore()
-        for shift in (-2, -1, 1, 2):
-
-            @pl.when((me + shift >= 0) & (me + shift < count))
+
+        def signal(device):
+            pl.semaphore_signal(
+                barrier, inc=1, device_id={"seq": lax.rem(device + count, count)},
+                device_id_type=pl.DeviceIdType.MESH,
+            )
+
+        for d in range(1, SHARE):
+            signal(base + peer_side(d))
+
+        @pl.when(place > 0)
+        def _():
+            signal(me - SHARE)
+
+            @pl.when(side == 0)
             def _():
-                pl.semaphore_signal(
-                    barrier, inc=1, device_id={"seq": lax.rem(me + shift + count, count)},
-                    device_id_type=pl.DeviceIdType.MESH,
-                )
-
-        pl.semaphore_wait(barrier, jnp.minimum(me, 2) + jnp.minimum(count - 1 - me, 2))
+                signal(me - 1)
+
+        @pl.when(place < places - 1)
+        def _():
+            signal(me + SHARE)
+
+            @pl.when(side == SHARE - 1)
+            def _():
+                signal(me + 1)
+
+        before, after = jnp.minimum(place, 1), jnp.minimum(places - 1 - place, 1)
+        peers = SHARE - 1 + before + after
+        peers += before * (1 - jnp.minimum(side, 1))
+        peers += after * (1 - jnp.minimum(SHARE - 1 - side, 1))
+        pl.semaphore_wait(barrier, peers)
 
         @pl.when(me < count - 1)
         def _():
@@ -177,12 +214,12 @@
         step = lax.broadcasted_iota(jnp.int32, (steps, tok), 0)
         token = lax.broadcasted_iota(jnp.int32, (steps, tok), 1)
         decay = decay_ref[...]
-        cum_buf[...] = exact(jnp.where(token * refl <= step, 1.0, 0.0), decay)
+        cum_buf[...] = exact_nt(jnp.where(token * refl <= step, 1.0, 0.0), decay)
         trow = lax.broadcasted_iota(jnp.int32, (tok, tok), 0)
         tcol = lax.broadcasted_iota(jnp.int32, (tok, tok), 1)
-        tok_buf[...] = exact(jnp.where(tcol <= trow, 1.0, 0.0), decay)
+        tok_buf[...] = exact_nt(jnp.where(tcol <= trow, 1.0, 0.0), decay)
         rate_buf[...] = sum(
-            exact(jnp.where(token * refl + j == step, 1.0, 0.0), rate_ref[:, j])
+            exact_nt(jnp.where(token * refl + j == step, 1.0, 0.0), rate_ref[j])
             for j in range(refl)
         )
 
@@ -302,19 +339,23 @@
             pb_ref[g, :, dim:] = pb[:, dim:]
 
         for j in range(own):
-            exchange(turn, j).start()
+            for d in range(1, SHARE):
+                exchange(turn, j, d).start()
+            other[(turn * own + j) * SHARE + side] = maps[here + first + j]
 
     @pl.when(turn > 0)
     def _():
         g = turn - 1
         joins = []
         for j in range(own):
-            exchange(g, j).wait_recv()
-            own_map, other_map = maps[g * group + first + j], other[g * own + j]
-            early = jnp.where(side == 0, own_map, other_map)
-            late = jnp.where(side == 0, other_map, own_map)
-            joined = mm_square(pair(early), late[:dim])
-            joins.append((joined[:dim], joined[dim:] + late[dim:], early))
+            for d in range(1, SHARE):
+                exchange(g, j, d, True).wait_recv()
+            joined = other[(g * own + j) * SHARE]
+            for n in range(1, SHARE):
+                late = other[(g * own + j) * SHARE + n]
+                product = mm_square(pair(joined), late[:dim])
+                joined = jnp.concatenate([product[:dim], product[dim:] + late[dim:]], 0)
+            joins.append((joined[:dim], joined[dim:]))
         rows = dim // PIECES
         for j in range(own):
             for piece in range(PIECES):
@@ -336,21 +377,26 @@
         for j in range(own):
             slot = g * own + j
             state = jnp.concatenate([recv[slot * PIECES + piece] for piece in range(PIECES)], 0)
-            early = joins[j][2]
-            later = mm_square(pair(state), early[:dim]) + early[dim:]
-            s_ref[g * group + first + j] = jnp.where(side == 0, state, later)
-            back[slot] = jnp.where(side == 0, later, state)
-            hand_back(g, j).start()
+            back[slot * SHARE] = state
+            for n in range(SHARE - 1):
+                step_map = other[slot * SHARE + n]
+                state = mm_square(pair(state), step_map[:dim]) + step_map[dim:]
+                back[slot * SHARE + n + 1] = state
+            for d in range(1, SHARE):
+                hand_back(g, j, d).start()
+            s_ref[g * group + first + j] = back[slot * SHARE + side]
 
     @pl.when(turn == parts)
     def _():
         @pl.loop(0, parts)
         def _(g):
             for j in range(own):
-                hand_back(g, j).wait_recv()
-                s_ref[g * group + rest + j] = mine[g * own + j]
-                exchange(g, j).wait_send()
-                hand_back(g, j).wait_send()
+                for d in range(1, SHARE):
+                    hand_back(g, j, d, True).wait_recv()
+                    head = g * group + peer_side(d) * own + j
+                    s_ref[head] = mine[head]
+                    exchange(g, j, d).wait_send()
+                    hand_back(g, j, d).wait_send()
 
         @pl.when(place < places - 1)
         def _():
@@ -362,15 +408,20 @@
 
 
 def out_kernel(pb_ref, s_ref, gate_ref, gain_ref, out_ref, buf):
-    heads, tok, dim = pb_ref.shape[0], pb_ref.shape[1], pb_ref.shape[2] // 2
-
-    @pl.loop(0, heads // GROUP)
-    def _(step):
-        for g in range(GROUP):
-            h = step * GROUP + g
-            value = mm_square(pair(pb_ref[h, :, :dim]), s_ref[h].T) + pb_ref[h, :, dim:]
-            buf[pl.ds(h, tok, stride=heads), :] = value
-
+    group, tok, dim = pb_ref.shape[0], pb_ref.shape[1], pb_ref.shape[2] // 2
+    heads = gate_ref.shape[1]
+    here = pl.program_id(0) * group
+    for g in range(group):
+        value = mm_square(pair(pb_ref[g, :, :dim]), s_ref[g].T) + pb_ref[g, :, dim:]
+        buf[pl.ds(here + g, tok, stride=heads), :] = value
+
+    @pl.when(pl.program_id(0) == pl.num_programs(0) - 1)
+    def _():
+        finish(buf, gate_ref, gain_ref, out_ref)
+
+
+def finish(buf, gate_ref, gain_ref, out_ref):
+    tok, heads, dim = gate_ref.shape
     rows = 8 * heads
 
     @pl.loop(0, tok // 8)
@@ -381,9 +432,6 @@
         out_ref[pl.ds(step * 8, 8)] = (normed * gain_ref[...] * gate).astype(out_ref.dtype)
 
 
-VMEM = pl.BlockSpec(memory_space=pltpu.VMEM)
-
-
 def one_prompt(q, k, v, rate, decay, gate, fq, fk, fv, gain):
     tok, heads, dim = q.shape
     refl = k.shape[1]
@@ -394,8 +442,8 @@
     def whole(shape):
         return pl.BlockSpec(shape, lambda i: (0,) * len(shape))
 
-    args = (q, k, v, fq, fk, fv, decay, rate)
-    half = heads // 2
+    args = (q, k, v, fq, fk, fv, decay.T, rate.transpose(1, 2, 0))
+    half = heads // SHARE
     rim = fq.shape[0] - 1
     dma = pltpu.SemaphoreType.DMA
     pb, states = pl.pallas_call(
@@ -423,13 +471,13 @@
             pltpu.VMEM((rim, refl, heads, dim), BF16),
             pltpu.VMEM((rim, refl, heads, dim), BF16),
             pltpu.VMEM((heads, 2 * dim, dim), F32),
-            pltpu.VMEM((half, 2 * dim, dim), F32),
+            pltpu.VMEM((half * SHARE, 2 * dim, dim), F32),
             pltpu.VMEM((half * PIECES, dim // PIECES, dim), F32),
             pltpu.VMEM((half * PIECES, dim // PIECES, dim), F32),
-            pltpu.VMEM((half, dim, dim), F32),
-            pltpu.VMEM((half, dim, dim), F32),
-            dma((3,)), dma((3,)), dma((half,)), dma((half,)),
-            dma((half * PIECES,)), dma((half * PIECES,)), dma((half,)), dma((half,)),
+            pltpu.VMEM((heads, dim, dim), F32),
+            pltpu.VMEM((heads, dim, dim), F32),
+            dma((3,)), dma((3,)), dma((heads,)), dma((heads,)),
+            dma((half * PIECES,)), dma((half * PIECES,)), dma((heads,)), dma((heads,)),
         ],
         compiler_params=pltpu.CompilerParams(
             collective_id=0, has_side_effects=True, vmem_limit_bytes=58 * 2**20
@@ -437,11 +485,17 @@
     )(*args)
     return pl.pallas_call(
         out_kernel,
-        in_specs=[VMEM] * 4,
-        out_specs=VMEM,
+        grid=(parts,),
+        in_specs=[
+            pl.BlockSpec((group, tok, 2 * dim), lambda i: (i, 0, 0)),
+            pl.BlockSpec((group, dim, dim), lambda i: (i, 0, 0)),
+            whole((tok, heads, dim)),
+            whole((heads, dim)),
+        ],
+        out_specs=whole((tok, heads, dim)),
         out_shape=jax.ShapeDtypeStruct((tok, heads, dim), BF16),
         scratch_shapes=[pltpu.VMEM((tok * heads, dim), F32)],
-        compiler_params=pltpu.CompilerParams(vmem_limit_bytes=32 * 2**20),
+        compiler_params=pltpu.CompilerParams(vmem_limit_bytes=58 * 2**20),
     )(pb, states, gate, gain)
 
 

time: 84 us -> 71.2 us (0.85)
  Pallas kernels: 77.9 us -> 71 us
  local copies, waits for them, and re-layouts: 5.77 us -> 0 us
    pallas_call x1, Pallas kernels: 73.8 us -> 64.7 us  [one_prompt(): pl.pallas_call(shard_kernel, grid=(parts + 1,), in_specs=[whole(x.shape)...]
    unnamed x10 -> x0, local copies, waits for them, and re-layouts: 5.77 us -> none
    pallas_call x1, Pallas kernels: 4.08 us -> 6.25 us  [one_prompt(): pl.pallas_call(out_kernel, grid=(parts,), in_specs=[pl.BlockSpec((group,...]
where the time goes in v4:
time: 71.2 us; the launch traced here: 71 us
  Pallas kernels  71 us (100%)
    pallas_call x1, Pallas kernels, one_prompt(): pl.pallas_call(shard_kernel, grid=(parts + 1,), in_specs=[whole(x.shape)...  64.7 us
    pallas_call x1, Pallas kernels, one_prompt(): pl.pallas_call(out_kernel, grid=(parts,), in_specs=[pl.BlockSpec((group,...  6.25 us

profile of v4, /device:TPU:29, one launch (start us, length us, event | category | flops | bytes accessed | tf_op | source)
XLA Modules:
  0.0 71.0 jit_solution(9629621143482109311)
XLA Ops:
  0.0 64.7 %shard_map.100 = (f32[16,128,256]{2,1,0:T(8,128)}, f32[16,128,128]{2,1,0:T(8,128)}) custom-call(bf16[128,16,128]{2,1,0:T(8,128)(2,1)} %bitcast.13, bf16[128,2,16,128]{3,2,1,0:T(8,128)(2,1)} %bitcast.11, bf16[128,2,16,128]{3,2,1,0:T(8,128)(2,1)} %bitcast.12, f32[4,16,128]{2,1,0:T(8,128)} %fq_ref.1, f32[4,2,16,128]{3,2,1,0:T(8,128)} %fk_ref.1, ...), custom_call_target="tpu_custom_call" | custom-call | tf_op jit(solution)/shard_map/pallas_call | solution.py:449
  64.7 6.3 %shard_map.101 = bf16[128,16,128]{2,1,0:T(8,128)(2,1)} custom-call(f32[16,128,256]{2,1,0:T(8,128)} %get-tuple-element.7.pb_ref, f32[16,128,128]{2,1,0:T(8,128)} %get-tuple-element.8.s_ref, bf16[128,16,128]{2,1,0:T(8,128)(2,1)} %bitcast.14, f32[16,128]{1,0:T(8,128)} %gain_ref.1), custom_call_target="tpu_custom_call" | custom-call | tf_op jit(solution)/shard_map/pallas_call | solution.py:486

commit v5 on v4

--- a/solution.py
+++ b/solution.py
@@ -74,7 +74,7 @@
             summed = summed + filter_ref[tap] * window[tap : tap + CHUNK]
         out = jax.nn.silu(summed)
         if normalize:
-            out = out / jnp.sqrt(jnp.sum(out * out, -1, keepdims=True) + epsilon)
+            out = out * lax.rsqrt(jnp.sum(out * out, -1, keepdims=True) + epsilon)
         buf[pl.ds(start, rows), :] = out.reshape(rows, out.shape[-1])
 
     if edge:
@@ -263,6 +263,7 @@
         col = lax.broadcasted_iota(jnp.int32, (half, half), 1)
         qrow = lax.broadcasted_iota(jnp.int32, (tok, steps), 0)
         qcol = lax.broadcasted_iota(jnp.int32, (tok, steps), 1)
+        apart = row ^ col
         eye = jnp.where(row == col, 1.0, 0.0)
         dim = q_ref.shape[2]
         drow = lax.broadcasted_iota(jnp.int32, (dim, dim), 0)
@@ -307,11 +308,11 @@
             work.append((low, low_21, mixing, right, keys_t, Q, cum_tok, last))
 
         inverse = [
-            [eye - jnp.where((row // 2) == (col // 2), low, 0.0) for low in item[0]] for item in work
+            [eye - jnp.where(apart < 2, low, 0.0) for low in item[0]] for item in work
         ]
         size = 2
         while size < half:
-            mask = ((row // (2 * size)) == (col // (2 * size))) & ((row // size) != (col // size))
+            mask = (apart >= size) & (apart < 2 * size)
             lefts = [[pair(x) for x in two] for two in inverse]
             inner = [
                 [
@@ -326,22 +327,26 @@
             ]
             size *= 2
 
+        outs = []
         for g, (item, two) in enumerate(zip(work, inverse)):
             low, low_21, mixing, right, keys_t, Q, cum_tok, last = item
             top = mm_wide(two[0], right[:half])
             bottom = mm_wide(two[1], right[half:] - mm_wide(low_21, top))
             solved = jnp.concatenate([top, bottom], 0)
             ab = mm_deep(keys_t, solved)
-            pb = mm_deep(mixing, solved)
             maps[here + g, :dim] = jnp.where(drow == dcol, jnp.exp(-last), 0.0) - ab[:, :dim].T
             maps[here + g, dim:] = ab[:, dim:].T
-            pb_ref[g, :, :dim] = jnp.exp(-cum_tok) * Q - pb[:, :dim]
-            pb_ref[g, :, dim:] = pb[:, dim:]
+            outs.append((mixing, solved, cum_tok, Q))
 
         for j in range(own):
             for d in range(1, SHARE):
                 exchange(turn, j, d).start()
             other[(turn * own + j) * SHARE + side] = maps[here + first + j]
+
+        for g, (mixing, solved, cum_tok, Q) in enumerate(outs):
+            pb = mm_deep(mixing, solved)
+            pb_ref[g, :, :dim] = jnp.exp(-cum_tok) * Q - pb[:, :dim]
+            pb_ref[g, :, dim:] = pb[:, dim:]
 
     @pl.when(turn > 0)
     def _():
@@ -427,7 +432,7 @@
     @pl.loop(0, tok // 8)
     def _(step):
         value = buf[pl.ds(pl.multiple_of(step * rows, rows), rows), :].reshape(8, heads, dim)
-        normed = value / jnp.sqrt(jnp.mean(value * value, -1, keepdims=True) + epsilon)
+        normed = value * lax.rsqrt(jnp.mean(value * value, -1, keepdims=True) + epsilon)
         gate = jax.nn.silu(gate_ref[pl.ds(step * 8, 8)].astype(F32))
         out_ref[pl.ds(step * 8, 8)] = (normed * gain_ref[...] * gate).astype(out_ref.dtype)
 

time: 71.2 us -> 68.9 us (0.968)
  Pallas kernels: 71 us -> 68.5 us
    pallas_call x1, Pallas kernels: 64.7 us -> 62.5 us  [one_prompt(): pl.pallas_call(shard_kernel, grid=(parts + 1,), in_specs=[whole(x.shape)...]
where the time goes in v5:
time: 68.9 us; the launch traced here: 68.5 us
  Pallas kernels  68.5 us (99%)
    pallas_call x1, Pallas kernels, one_prompt(): pl.pallas_call(shard_kernel, grid=(parts + 1,), in_specs=[whole(x.shape)...  62.5 us
    pallas_call x1, Pallas kernels, one_prompt(): pl.pallas_call(out_kernel, grid=(parts,), in_specs=[pl.BlockSpec((group,...  6.01 us

profile of v5, /device:TPU:29, one launch (start us, length us, event | category | flops | bytes accessed | tf_op | source)
XLA Modules:
  0.0 68.5 jit_solution(9394049985876044794)
XLA Ops:
  0.0 62.5 %shard_map.100 = (f32[16,128,256]{2,1,0:T(8,128)}, f32[16,128,128]{2,1,0:T(8,128)}) custom-call(bf16[128,16,128]{2,1,0:T(8,128)(2,1)} %bitcast.13, bf16[128,2,16,128]{3,2,1,0:T(8,128)(2,1)} %bitcast.11, bf16[128,2,16,128]{3,2,1,0:T(8,128)(2,1)} %bitcast.12, f32[4,16,128]{2,1,0:T(8,128)} %fq_ref.1, f32[4,2,16,128]{3,2,1,0:T(8,128)} %fk_ref.1, ...), custom_call_target="tpu_custom_call" | custom-call | tf_op jit(solution)/shard_map/pallas_call | solution.py:454
  62.5 6.0 %shard_map.101 = bf16[128,16,128]{2,1,0:T(8,128)(2,1)} custom-call(f32[16,128,256]{2,1,0:T(8,128)} %get-tuple-element.7.pb_ref, f32[16,128,128]{2,1,0:T(8,128)} %get-tuple-element.8.s_ref, bf16[128,16,128]{2,1,0:T(8,128)(2,1)} %bitcast.14, f32[16,128]{1,0:T(8,128)} %gain_ref.1), custom_call_target="tpu_custom_call" | custom-call | tf_op jit(solution)/shard_map/pallas_call | solution.py:491
